TPU v7x, 32 devices: a whole 2x2x4 slice. The times are simulated.
32 devices in a mesh: chan: 16 (over z, y, x), blk: 2 (over core).
Axes of the slice: x: 2, y: 2, z: 4, core: 2. Of those that a mesh axis runs over, the one named last changes fastest.
Arguments:
- amps: bfloat16 [16, 1024, 1024], P('chan', 'blk'), may hold values from -6 to 6
- six_j: bfloat16 [16, 1024, 1024], P('chan'), may hold values from -0.1875 to 0.1875
- interaction: bfloat16 [16, 1024, 1024], P('chan', 'blk'), may hold values from -0.1875 to 0.1875
- deal: int32 [16], replicated, may hold values from 0 to 15, each once
- pandya_map: int32 [16], replicated, may hold values from 0 to 15, each once
- rows_live: int32 [16], replicated, may hold values from 1 to 1024, 8192 in all
Outputs:
- update: bfloat16 [16, 1024, 1024], P('chan', 'blk')
Inputs may be any that keep to these rules, and one draw needn't show every extreme that they name: `deal`: each channel once. `pandya_map`: each channel once. `rows_live`: the counts sum to 16 * 1024 // 2.
All inputs are finite; a program needn't handle non-finite values.
Results may differ from a plain program's by a relative error of at most 0.0057.
Values may be sent and summed in bfloat16 or wider, within the bound.
No kernel may reach another device: no remote copies, remote signals or barrier semaphores. Data moves between devices by JAX's collectives and lax.ppermute only.
A program may use at most 64 MiB of HBM per device.

v0:
```python
import jax
import jax.numpy as jnp
from jax import lax
from jax.sharding import PartitionSpec as P


def column_index(order, width):
    offsets = jnp.arange(width, dtype=jnp.int32)
    return (order[:, None] * width + offsets[None, :]).reshape(-1)


def selector(source_cols, cols):
    sources = jnp.arange(cols, dtype=jnp.int32)
    return (sources[:, None] == source_cols[None, :]).astype(jnp.bfloat16)


def per_device(amps, six_j, interaction, deal, pandya_map, rows_live):
    groups = lax.axis_size("chan")
    row_count = amps.shape[1]
    cols = amps.shape[2]
    width = cols // groups
    slot = lax.axis_index("chan")
    first_row = lax.axis_index("blk") * row_count
    live = lax.dynamic_slice_in_dim(rows_live, slot, 1, 0)[0]
    row_ids = first_row + jnp.arange(row_count, dtype=jnp.int32)
    keep = (row_ids < live).astype(jnp.bfloat16)[:, None]
    inv_map = jnp.argsort(pandya_map)
    send_select = selector(column_index(inv_map, width), cols)
    outgoing = jnp.dot(amps[0] * keep, send_select, preferred_element_type=jnp.float32).astype(
        jnp.bfloat16
    )
    incoming = lax.all_to_all(outgoing, "chan", split_axis=1, concat_axis=1, tiled=True)
    six_rows = jnp.take(six_j[0], column_index(deal, width), axis=0)
    coupled = jnp.dot(incoming, six_rows, preferred_element_type=jnp.float32).astype(jnp.bfloat16)
    whole_panel = lax.all_gather(interaction, "blk", axis=1, tiled=True)[0]
    dressed_sum = jnp.dot(coupled, whole_panel, preferred_element_type=jnp.float32)
    dressed = dressed_sum.astype(jnp.bfloat16)
    sending = lax.dot_general(
        dressed, six_rows, (((1,), (1,)), ((), ())), preferred_element_type=jnp.float32
    ).astype(jnp.bfloat16)
    arriving = lax.all_to_all(sending, "chan", split_axis=1, concat_axis=1, tiled=True)
    back_select = selector(column_index(pandya_map, width), cols)
    result = (
        jnp.dot(arriving, back_select, preferred_element_type=jnp.float32).astype(jnp.bfloat16)
        * keep
    )
    return result.reshape(1, row_count, cols)


def solution(mesh):
    in_specs = (
        P("chan", "blk", None),
        P("chan", None, None),
        P("chan", "blk", None),
        P(),
        P(),
        P(),
    )
    out_specs = P("chan", "blk", None)
    return jax.shard_map(
        per_device, mesh=mesh, in_specs=in_specs, out_specs=out_specs, check_vma=False
    )
```

profile of v0, /device:TPU:0, one launch (start us, length us, event | category | flops | bytes accessed | tf_op | source)
XLA Modules:
  0.0 96.1 jit_solution(18094539102324854481)
XLA Ops:
  6.5 0.7 all-gather.2.cloned.1.call-update
  7.3 1.9 %sort.17 = (s32[16]{0:T(128)}, s32[16]{0:T(128)S(1)}) sort(s32[16]{0:T(128)} %param.10, s32[16]{0:T(128)S(1)} %iota.23), dimensions={0}, to_apply=%region_0.0 | sort | flops 64 | bytes 256 | tf_op jit(solution)/shard_map/jit(argsort)/sort | solution.py:27
  9.2 0.1 iota_add_fusion.2
  9.2 0.1 add.109
  9.3 1.2 %dynamic_slice.3 = s32[1]{0:T(128)} dynamic-slice(s32[16]{0:T(128)} %param.11, s32[]{:T(128)S(6)} %select_n.23), dynamic_slice_sizes={1} | dynamic-slice | bytes 12 | tf_op jit(solution)/shard_map/dynamic_slice | solution.py:24
  10.6 0.6 fusion.14
  11.2 2.6 %fusion.10 = bf16[512,1024]{1,0:T(8,128)(2,1)S(1)} fusion(s32[1024]{0:T(1024)S(1)} %add.109, bf16[1,512,1024]{2,1,0:T(8,128)(2,1)} %param.6, bf16[512]{0:T(512)(128)(2,1)S(1)} %fusion.14), kind=kOutput, calls=%fused_computation.12 | convolution fusion | flops 1075838976 | bytes 2102272 | tf_op jit(solution)/shard_map/dot_general | solution.py:29
  13.8 0.0 copy-start.1
  13.8 1.3 %copy.7 = bf16[512,1024]{0,1:T(8,128)(2,1)} copy(bf16[512,1024]{1,0:T(8,128)(2,1)S(1)} %fusion.10) | data formatting | bytes 2097152 | tf_op jit(solution)/shard_map/convert_element_type | solution.py:29
  15.1 8.3 %all-to-all-start = ((bf16[512,16,64]{0,2,1:T(8,128)(2,1)}), bf16[512,16,64]{0,2,1:T(8,128)(2,1)S(1)}, u32[]{:S(2)}, u32[]{:S(2)}) async-start(bf16[512,16,64]{0,2,1:T(8,128)(2,1)} %bitcast.2), calls=%async_computation | async-start | bytes 2097152 | tf_op jit(solution)/shard_map/all_to_all | solution.py:32
  23.5 0.1 iota_add_fusion.1
  23.6 0.1 add.116
  23.6 0.1 add.113
  23.7 5.4 %gather_fusion = bf16[1024,1024]{1,0:T(8,128)(2,1)} fusion(bf16[1024,1024]{1,0:T(8,128)(2,1)S(1)} %bitcast.20, s32[1024]{0:T(1024)S(1)} %broadcast_clamp_fusion), kind=kCustom, calls=%fused_computation | custom fusion | bytes 4198400 | tf_op jit(solution)/shard_map/jit(_take)/gather | solution.py:33
  29.1 18.8 %all-to-all-done = bf16[512,16,64]{0,2,1:T(8,128)(2,1)S(1)} async-done(((bf16[512,16,64]{0,2,1:T(8,128)(2,1)}), bf16[512,16,64]{0,2,1:T(8,128)(2,1)S(1)}, u32[]{:S(2)}, u32[]{:S(2)}) %all-to-all-start) | async-done | bytes 1048608 | tf_op jit(solution)/shard_map/all_to_all | solution.py:32
  47.9 5.6 %fusion.6 = bf16[512,1024]{1,0:T(8,128)(2,1)} fusion(bf16[1,1024,1024]{2,1,0:T(8,128)(2,1)} %all-gather.2.cloned.1.call-done, bf16[512,1024]{0,1:T(8,128)(2,1)S(1)} %bitcast.21, bf16[1024,1024]{1,0:T(8,128)(2,1)} %gather_fusion, pred[1024]{0:T(1024)(128)(4,1)S(1)} %compare_and_fusion), kind=kOutput, calls=%fused_computation.10 | convolution fusion | flops 2149580800 | bytes 6292480 | tf_op jit(solution)/shard_map/dot_general | solution.py:36
  53.5 3.3 %convolution_convert_fusion = bf16[512,1024]{1,0:T(8,128)(2,1)S(1)} fusion(bf16[512,1024]{1,0:T(8,128)(2,1)} %fusion.6, bf16[1024,1024]{1,0:T(8,128)(2,1)} %gather_fusion, pred[1024]{0:T(1024)(128)(4,1)S(1)} %compare_and_fusion), kind=kOutput, calls=%fused_computation.13 | convolution fusion | flops 1075314688 | bytes 4195328 | tf_op jit(solution)/shard_map/dot_general | solution.py:38
  56.8 0.0 copy-start.2
  56.8 1.3 %copy.8 = bf16[512,1024]{0,1:T(8,128)(2,1)} copy(bf16[512,1024]{1,0:T(8,128)(2,1)S(1)} %convolution_convert_fusion) | data formatting | bytes 2097152 | tf_op jit(solution)/shard_map/convert_element_type | solution.py:40
  58.2 5.8 %all-to-all-start.1 = ((bf16[512,16,64]{0,2,1:T(8,128)(2,1)}), bf16[512,16,64]{0,2,1:T(8,128)(2,1)S(1)}, u32[]{:S(2)}, u32[]{:S(2)}) async-start(bf16[512,16,64]{0,2,1:T(8,128)(2,1)} %bitcast.7), calls=%async_computation.1 | async-start | bytes 2097152 | tf_op jit(solution)/shard_map/all_to_all | solution.py:41
  64.0 0.1 iota_add_fusion
  64.1 0.1 add.122
  64.2 22.8 %all-to-all-done.1 = bf16[512,16,64]{0,2,1:T(8,128)(2,1)S(1)} async-done(((bf16[512,16,64]{0,2,1:T(8,128)(2,1)}), bf16[512,16,64]{0,2,1:T(8,128)(2,1)S(1)}, u32[]{:S(2)}, u32[]{:S(2)}) %all-to-all-start.1) | async-done | bytes 1048608 | tf_op jit(solution)/shard_map/all_to_all | solution.py:41
  87.0 2.3 %fusion.12 = bf16[1,512,1024]{2,1,0:T(8,128)(2,1)} fusion(bf16[512,1024]{0,1:T(8,128)(2,1)S(1)} %bitcast.22, s32[1024]{0:T(1024)S(1)} %add.122, bf16[512]{0:T(512)(128)(2,1)S(1)} %fusion.14), kind=kOutput, calls=%fused_computation.16 | convolution fusion | flops 1075838976 | bytes 2102272 | tf_op jit(solution)/shard_map/dot_general | solution.py:44
  (13 shorter events, 0.0 us)
Async XLA Ops:
  6.5 17.2 %copy-start = (bf16[1,1024,1024]{2,1,0:T(8,128)(2,1)S(1)}, bf16[1,1024,1024]{2,1,0:T(8,128)(2,1)}, u32[]{:S(2)}) copy-start(bf16[1,1024,1024]{2,1,0:T(8,128)(2,1)} %param.7) | copy-start | bytes 6291460
  6.5 41.4 %all-gather.2.cloned.1.call-start = ((), (), s32[]{:S(2)}) async-start(), calls=%async_computation.2 | async-start | bytes 3145728 | tf_op jit(solution)/shard_map/all_gather | solution.py:35
  13.8 9.7 %copy-start.1 = (s32[16]{0:T(128)S(1)}, s32[16]{0:T(128)}, u32[]{:S(2)}) copy-start(s32[16]{0:T(128)} %param.9) | copy-start | bytes 196
  15.1 32.8 %all-to-all-start = ((bf16[512,16,64]{0,2,1:T(8,128)(2,1)}), bf16[512,16,64]{0,2,1:T(8,128)(2,1)S(1)}, u32[]{:S(2)}, u32[]{:S(2)}) async-start(bf16[512,16,64]{0,2,1:T(8,128)(2,1)} %bitcast.2), calls=%async_computation | async-start | bytes 2097152 | tf_op jit(solution)/shard_map/all_to_all | solution.py:32
  56.8 7.2 %copy-start.2 = (s32[16]{0:T(128)S(1)}, s32[16]{0:T(128)}, u32[]{:S(2)}) copy-start(s32[16]{0:T(128)} %param.10) | copy-start | bytes 196
  58.2 28.8 %all-to-all-start.1 = ((bf16[512,16,64]{0,2,1:T(8,128)(2,1)}), bf16[512,16,64]{0,2,1:T(8,128)(2,1)S(1)}, u32[]{:S(2)}, u32[]{:S(2)}) async-start(bf16[512,16,64]{0,2,1:T(8,128)(2,1)} %bitcast.7), calls=%async_computation.1 | async-start | bytes 2097152 | tf_op jit(solution)/shard_map/all_to_all | solution.py:41
Sparse Core Ops, SparseCore 0:
  8.9 13.2 all-gather.1
where the time goes:
time: 96.5 us; the launch traced here: 96.1 us
  waiting for transfers between devices  42.3 us (44%)
  starting transfers between devices  14.1 us (15%)
  matrix products  13.8 us (14%)
  between operations  13.5 us (14%)
  local copies, waits for them, and re-layouts  9.6 us (10%)
  other arithmetic  2.79 us (3%)
    all_to_all x1, waiting for transfers between devices, per_device(): lax.all_to_all(sending, 'chan', split_axis=1, concat_axis=1, tiled=True)  22.8 us
    all_to_all x1, waiting for transfers between devices, per_device(): lax.all_to_all(outgoing, 'chan', split_axis=1, concat_axis=1, tiled=True)  18.8 us
    all_to_all x1, starting transfers between devices, per_device(): lax.all_to_all(outgoing, 'chan', split_axis=1, concat_axis=1, tiled=True)  8.31 us
    all_to_all x1, starting transfers between devices, per_device(): lax.all_to_all(sending, 'chan', split_axis=1, concat_axis=1, tiled=True)  5.82 us
    dot_general x1, matrix products, per_device(): jnp.dot(coupled, whole_panel, preferred_element_type=jnp.float32)  5.63 us
    gather x1, local copies, waits for them, and re-layouts, per_device(): six_rows = jnp.take(six_j[0], column_index(deal, width), axis=0)  5.4 us
    dot_general x1, matrix products, per_device(): lax.dot_general(dressed, six_rows, (((1,), (1,)), ((), ())), preferred_el...  3.28 us
    dot_general x1, matrix products, per_device(): jnp.dot(amps[0] * keep, send_select, preferred_element_type=jnp.float32)  2.58 us
  transfers between devices with their start and end apart: 3, of which 2 were waited for; matrix products, arithmetic and copies ran while one was open for 14% of the time, Pallas kernels for 0%

commit v1 on v0

v1 whole, which is shorter than its diff:
```python
import functools

import jax
import jax.numpy as jnp
from jax import lax
from jax.experimental import pallas as pl
from jax.experimental.pallas import tpu as pltpu
from jax.sharding import PartitionSpec as P

LANES = 128


def live_lanes(first, rows, live):
    ids = first + lax.broadcasted_iota(jnp.int32, (LANES, rows), 1)
    return ids < live


def scatter_kernel(width, map_ref, live_ref, amps_ref, out_ref, tile, turned, in_sem, out_sem):
    rows, cols = amps_ref.shape
    slot = lax.axis_index("chan")
    first = lax.axis_index("blk") * rows
    live = live_ref[slot]
    tiles = cols // LANES
    per_tile = LANES // width
    loads = [
        pltpu.make_async_copy(
            amps_ref.at[:, pl.ds(j * LANES, LANES)], tile.at[j], in_sem.at[j]
        )
        for j in range(tiles)
    ]
    for load in loads:
        load.start()
    keep = live_lanes(first, rows, live)
    stores = []
    for j in range(tiles):
        loads[j].wait()
        turned[pl.ds(j * LANES, LANES), :] = jnp.where(keep, tile[j].T, 0)
        for i in range(per_tile):
            k = j * per_tile + i
            store = pltpu.make_async_copy(
                turned.at[pl.ds(k * width, width), :],
                out_ref.at[pl.ds(pl.multiple_of(map_ref[k] * width, width), width), :],
                out_sem.at[k],
            )
            store.start()
            stores.append(store)
    for store in stores:
        store.wait()


def gather_kernel(width, map_ref, live_ref, back_ref, out_ref, turned, tile, in_sem, out_sem):
    rows, cols = out_ref.shape
    slot = lax.axis_index("chan")
    first = lax.axis_index("blk") * rows
    live = live_ref[slot]
    tiles = cols // LANES
    per_tile = LANES // width
    loads = [
        pltpu.make_async_copy(
            back_ref.at[pl.ds(pl.multiple_of(map_ref[k] * width, width), width), :],
            turned.at[pl.ds(k * width, width), :],
            in_sem.at[k],
        )
        for k in range(cols // width)
    ]
    for load in loads:
        load.start()
    keep = live_lanes(first, rows, live)
    stores = []
    for j in range(tiles):
        for i in range(per_tile):
            loads[j * per_tile + i].wait()
        tile[j] = jnp.where(keep, turned[pl.ds(j * LANES, LANES), :], 0).T
        store = pltpu.make_async_copy(
            tile.at[j], out_ref.at[:, pl.ds(j * LANES, LANES)], out_sem.at[j]
        )
        store.start()
        stores.append(store)
    for store in stores:
        store.wait()


def move(kernel, out_shape, width, pandya_map, rows_live, block):
    cols, rows = out_shape if kernel is scatter_kernel else block.shape
    tile = pltpu.VMEM((cols // LANES, rows, LANES), jnp.bfloat16)
    turned = pltpu.VMEM((cols, rows), jnp.bfloat16)
    tile_sem = pltpu.SemaphoreType.DMA((cols // LANES,))
    group_sem = pltpu.SemaphoreType.DMA((cols // width,))
    if kernel is scatter_kernel:
        scratch = [tile, turned, tile_sem, group_sem]
    else:
        scratch = [turned, tile, group_sem, tile_sem]
    return pl.pallas_call(
        functools.partial(kernel, width),
        out_shape=jax.ShapeDtypeStruct(out_shape, jnp.bfloat16),
        in_specs=[
            pl.BlockSpec(memory_space=pltpu.SMEM),
            pl.BlockSpec(memory_space=pltpu.SMEM),
            pl.BlockSpec(memory_space=pl.ANY),
        ],
        out_specs=pl.BlockSpec(memory_space=pl.ANY),
        scratch_shapes=scratch,
        cost_estimate=pl.CostEstimate(
            flops=0, bytes_accessed=4 * cols * rows, transcendentals=0
        ),
    )(pandya_map, rows_live, block)


def per_device(amps, six_j, interaction, deal, pandya_map, rows_live):
    groups = lax.axis_size("chan")
    _, rows, cols = amps.shape
    width = cols // groups
    whole = lax.all_gather(interaction, "blk", axis=1, tiled=True)[0]
    outgoing = move(scatter_kernel, (cols, rows), width, pandya_map, rows_live, amps[0])
    incoming = lax.all_to_all(
        outgoing.reshape(groups, width, rows), "chan", split_axis=0, concat_axis=0, tiled=True
    )
    six = six_j[0].reshape(groups, width, cols)[deal].reshape(cols, cols)
    right = lax.dot_general(
        whole, six, (((1,), (1,)), ((), ())), preferred_element_type=jnp.float32
    ).astype(jnp.bfloat16)
    both = lax.dot_general(
        right, six, (((0,), (1,)), ((), ())), preferred_element_type=jnp.float32
    ).astype(jnp.bfloat16)
    sending = jnp.dot(
        both, incoming.reshape(cols, rows), preferred_element_type=jnp.float32
    ).astype(jnp.bfloat16)
    arriving = lax.all_to_all(
        sending.reshape(groups, width, rows), "chan", split_axis=0, concat_axis=0, tiled=True
    )
    result = move(
        gather_kernel, (rows, cols), width, pandya_map, rows_live, arriving.reshape(cols, rows)
    )
    return result[None]


def solution(mesh):
    in_specs = (
        P("chan", "blk", None),
        P("chan", None, None),
        P("chan", "blk", None),
        P(),
        P(),
        P(),
    )
    out_specs = P("chan", "blk", None)
    return jax.shard_map(
        per_device, mesh=mesh, in_specs=in_specs, out_specs=out_specs, check_vma=False
    )
```

time: 96.5 us -> 91.3 us (0.946)
  blocking collectives: 0 us -> 30.9 us
  waiting for transfers between devices: 42.3 us -> 17.2 us
  local copies, waits for them, and re-layouts: 9.6 us -> 2 us
  Pallas kernels: 0 us -> 6.45 us
  starting transfers between devices: 14.1 us -> 8.33 us
  other arithmetic: 2.79 us -> 0.01 us
  matrix products: 13.8 us -> 12.6 us
    all_to_all x0 -> x1, blocking collectives: none -> 30.9 us  [per_device(): lax.all_to_all(sending.reshape(groups, width, rows), 'chan', split_axis=0...]
    all_to_all x2 -> x1, waiting for transfers between devices: 41.6 us -> 15.2 us  [per_device(): lax.all_to_all(outgoing.reshape(groups, width, rows), 'chan', split_axis=...]
    pallas_call x0 -> x2, Pallas kernels: none -> 6.45 us  [move(): pl.pallas_call(functools.partial(kernel, width), out_shape=jax.ShapeDtype...]
    all_to_all x2 -> x1, starting transfers between devices: 14.1 us -> 8.32 us  [per_device(): lax.all_to_all(outgoing.reshape(groups, width, rows), 'chan', split_axis=...]
    gather x1, local copies, waits for them, and re-layouts: 5.4 us -> 1.99 us  [per_device(): six = six_j[0].reshape(groups, width, cols)[deal].reshape(cols, cols)]
    convert_element_type x2 -> x0, local copies, waits for them, and re-layouts: 2.65 us -> none  [the longest x1 1.32 us: per_device(): jnp.dot(amps[0] * keep, send_select, preferred_element_type=jnp.float32)]
    sort x1 -> x0, other arithmetic: 1.9 us -> none  [per_device(): inv_map = jnp.argsort(pandya_map)]
    all_gather x1, waiting for transfers between devices: 0.01 us -> 1.27 us  [per_device(): whole = lax.all_gather(interaction, 'blk', axis=1, tiled=True)[0]]
  transfers between devices with their start and end apart: 3 -> 2, of which waited for: 2 -> 2; matrix products, arithmetic and copies ran while one was open for 14% -> 9% of each run, Pallas kernels for 0% -> 4%
where the time goes in v1:
time: 91.3 us; the launch traced here: 90.9 us
  blocking collectives  30.9 us (34%)
  waiting for transfers between devices  17.2 us (19%)
  between operations  13.5 us (15%)
  matrix products  12.6 us (14%)
  starting transfers between devices  8.33 us (9%)
  Pallas kernels  6.45 us (7%)
  local copies, waits for them, and re-layouts  2 us (2%)
    all_to_all x1, blocking collectives, per_device(): lax.all_to_all(sending.reshape(groups, width, rows), 'chan', split_axis=0...  30.9 us
    all_to_all x1, waiting for transfers between devices, per_device(): lax.all_to_all(outgoing.reshape(groups, width, rows), 'chan', split_axis=...  15.2 us
    all_to_all x1, starting transfers between devices, per_device(): lax.all_to_all(outgoing.reshape(groups, width, rows), 'chan', split_axis=...  8.32 us
    dot_general x1, matrix products, per_device(): jnp.dot(both, incoming.reshape(cols, rows), preferred_element_type=jnp.fl...  6.65 us
    pallas_call x2, Pallas kernels, move(): pl.pallas_call(functools.partial(kernel, width), out_shape=jax.ShapeDtype...  6.45 us
    dot_general x1, matrix products, per_device(): lax.dot_general(whole, six, (((1,), (1,)), ((), ())), preferred_element_t...  5.91 us
    gather x1, local copies, waits for them, and re-layouts, per_device(): six = six_j[0].reshape(groups, width, cols)[deal].reshape(cols, cols)  1.99 us
  transfers between devices with their start and end apart: 2, of which 2 were waited for; matrix products, arithmetic and copies ran while one was open for 9% of the time, Pallas kernels for 4%

profile of v1, /device:TPU:0, one launch (start us, length us, event | category | flops | bytes accessed | tf_op | source)
XLA Modules:
  0.0 90.9 jit_solution(6869427272342038435)
XLA Ops:
  6.5 0.0 copy-start
  6.5 0.0 all-gather.2.cloned.1.call-start
  6.5 0.7 all-gather.2.cloned.1.call-update
  7.3 0.0 copy-start.1
  7.3 3.3 %shard_map.64 = bf16[1024,512]{1,0:T(8,128)(2,1)} custom-call(s32[16]{0:T(128)} %map_ref.3, s32[16]{0:T(128)} %live_ref.3, bf16[512,1024]{1,0:T(8,128)(2,1)} %bitcast.22), custom_call_target="tpu_custom_call" | custom-call | bytes 2097152 | tf_op jit(solution)/shard_map/pallas_call | solution.py:93
  10.6 8.3 %all-to-all-start = ((bf16[16,64,512]{2,1,0:T(8,128)(2,1)}), bf16[16,64,512]{2,1,0:T(8,128)(2,1)S(1)}, u32[]{:S(2)}, u32[]{:S(2)}) async-start(bf16[16,64,512]{2,1,0:T(8,128)(2,1)} %bitcast.16), calls=%async_computation | async-start | bytes 2097152 | tf_op jit(solution)/shard_map/all_to_all | solution.py:115
  18.9 0.0 copy-done.1
  18.9 0.0 copy-done
  18.9 2.0 %gather_fusion = bf16[16,64,1024]{2,1,0:T(8,128)(2,1)} fusion(bf16[16,64,1024]{2,1,0:T(8,128)(2,1)S(1)} %bitcast.15, s32[1024]{0:T(1024)S(1)} %pad_clamp_fusion), kind=kCustom, calls=%fused_computation | custom fusion | bytes 4194368 | tf_op jit(solution)/shard_map/gather | solution.py:118
  20.9 1.3 %all-gather.2.cloned.1.call-done = bf16[1,1024,1024]{2,1,0:T(8,128)(2,1)} async-done(((bf16[1,512,1024]{2,1,0:T(8,128)(2,1)}), bf16[1,1024,1024]{2,1,0:T(8,128)(2,1)}) %all-gather.2.cloned.1.call-update) | async-done | bytes 2097168 | tf_op jit(solution)/shard_map/all_gather | solution.py:113
  22.2 5.9 %fusion = bf16[1024,1024]{1,0:T(8,128)(2,1)} fusion(bf16[1024,1024]{1,0:T(8,128)(2,1)} %bitcast.18, bf16[1,1024,1024]{2,1,0:T(8,128)(2,1)} %all-gather.2.cloned.1.call-done), kind=kOutput, calls=%fused_computation.1 | convolution fusion | flops 2147483648 | bytes 6291456 | tf_op jit(solution)/shard_map/dot_general | solution.py:119
  28.1 15.2 %all-to-all-done = bf16[16,64,512]{2,1,0:T(8,128)(2,1)S(1)} async-done(((bf16[16,64,512]{2,1,0:T(8,128)(2,1)}), bf16[16,64,512]{2,1,0:T(8,128)(2,1)S(1)}, u32[]{:S(2)}, u32[]{:S(2)}) %all-to-all-start) | async-done | bytes 1048608 | tf_op jit(solution)/shard_map/all_to_all | solution.py:115
  43.3 6.6 %fusion.6 = bf16[1024,512]{1,0:T(8,128)(2,1)} fusion(bf16[1024,512]{1,0:T(8,128)(2,1)S(1)} %bitcast.20, bf16[1024,1024]{1,0:T(8,128)(2,1)} %bitcast.19, bf16[1024,1024]{1,0:T(8,128)(2,1)} %fusion), kind=kOutput, calls=%fused_computation.7 | convolution fusion | flops 3222798336 | bytes 6291456 | tf_op jit(solution)/shard_map/dot_general | solution.py:125
  50.0 30.9 %all_to_all.10 = bf16[16,64,512]{2,1,0:T(8,128)(2,1)} all-to-all(bf16[16,64,512]{2,1,0:T(8,128)(2,1)} %bitcast.21), channel_id=1, replica_groups=mesh['chan'=16,'blk'=2] {'chan'}, dimensions={0} | all-to-all | bytes 2097152 | tf_op jit(solution)/shard_map/all_to_all | solution.py:128
  80.9 3.2 %shard_map.65 = bf16[512,1024]{1,0:T(8,128)(2,1)} custom-call(s32[16]{0:T(128)} %map_ref.3, s32[16]{0:T(128)} %live_ref.3, bf16[1024,512]{1,0:T(8,128)(2,1)} %bitcast.17), custom_call_target="tpu_custom_call" | custom-call | bytes 2097152 | tf_op jit(solution)/shard_map/pallas_call | solution.py:93
  (2 shorter events, 0.0 us)
Async XLA Ops:
  6.5 12.4 %copy-start = (bf16[1,1024,1024]{2,1,0:T(8,128)(2,1)S(1)}, bf16[1,1024,1024]{2,1,0:T(8,128)(2,1)}, u32[]{:S(2)}) copy-start(bf16[1,1024,1024]{2,1,0:T(8,128)(2,1)} %param.7) | copy-start | bytes 6291460
  6.5 15.7 %all-gather.2.cloned.1.call-start = ((), (), s32[]{:S(2)}) async-start(), calls=%async_computation.2 | async-start | bytes 3145728 | tf_op jit(solution)/shard_map/all_gather | solution.py:113
  7.3 11.6 %copy-start.1 = (s32[16]{0:T(128)S(1)}, s32[16]{0:T(128)}, u32[]{:S(2)}) copy-start(s32[16]{0:T(128)} %param.9) | copy-start | bytes 196
  10.6 32.8 %all-to-all-start = ((bf16[16,64,512]{2,1,0:T(8,128)(2,1)}), bf16[16,64,512]{2,1,0:T(8,128)(2,1)S(1)}, u32[]{:S(2)}, u32[]{:S(2)}) async-start(bf16[16,64,512]{2,1,0:T(8,128)(2,1)} %bitcast.16), calls=%async_computation | async-start | bytes 2097152 | tf_op jit(solution)/shard_map/all_to_all | solution.py:115
Sparse Core Ops, SparseCore 0:
  8.9 13.2 all-gather.1

commit v2 on v1

--- a/solution.py
+++ b/solution.py
@@ -106,22 +106,85 @@
     )(pandya_map, rows_live, block)
 
 
+def chain_kernel(width, deal_ref, six_ref, panel_ref, out_ref, six, panel, right, six_sem, panel_sem):
+    cols = six.shape[0]
+    fetch = [
+        pltpu.make_async_copy(
+            six_ref.at[pl.ds(pl.multiple_of(deal_ref[s] * width, width), width), :],
+            six.at[pl.ds(s * width, width), :],
+            six_sem.at[s],
+        )
+        for s in range(cols // width)
+    ]
+    fetch_panel = pltpu.make_async_copy(panel_ref, panel, panel_sem)
+    fetch_panel.start()
+    for copy in fetch:
+        copy.start()
+    for copy in fetch:
+        copy.wait()
+    fetch_panel.wait()
+    step = min(256, cols)
+    across = (((1,), (1,)), ((), ()))
+
+    @pl.loop(0, cols // step)
+    def _(i):
+        at = pl.ds(pl.multiple_of(i * step, step), step)
+        right[at, :] = lax.dot_general(
+            six[at, :], panel[...], across, preferred_element_type=jnp.float32
+        ).astype(jnp.bfloat16)
+        out_ref[at, :] = lax.dot_general(
+            right[at, :], six[...], across, preferred_element_type=jnp.float32
+        ).astype(jnp.bfloat16)
+
+
+def chain(width, deal, six, panel):
+    cols = six.shape[0]
+    square = pltpu.VMEM((cols, cols), jnp.bfloat16)
+    return pl.pallas_call(
+        functools.partial(chain_kernel, width),
+        out_shape=jax.ShapeDtypeStruct((cols, cols), jnp.bfloat16),
+        in_specs=[
+            pl.BlockSpec(memory_space=pltpu.SMEM),
+            pl.BlockSpec(memory_space=pl.ANY),
+            pl.BlockSpec(memory_space=pl.ANY),
+        ],
+        out_specs=pl.BlockSpec(memory_space=pltpu.VMEM),
+        scratch_shapes=[
+            square,
+            square,
+            square,
+            pltpu.SemaphoreType.DMA((cols // width,)),
+            pltpu.SemaphoreType.DMA,
+        ],
+        compiler_params=pltpu.CompilerParams(vmem_limit_bytes=24 * 1024 * 1024),
+        cost_estimate=pl.CostEstimate(
+            flops=4 * cols**3, bytes_accessed=6 * cols * cols, transcendentals=0
+        ),
+    )(deal, six, panel)
+
+
+def whole_panel(part):
+    shares = lax.axis_size("blk")
+    me = lax.axis_index("blk")
+    rows, cols = part.shape
+    whole = jnp.zeros((shares * rows, cols), part.dtype)
+    for step in range(shares):
+        owner = lax.rem(me + shares - step, shares)
+        whole = lax.dynamic_update_slice(whole, part, (owner * rows, 0))
+        if step < shares - 1:
+            part = lax.ppermute(part, "blk", [(i, (i + 1) % shares) for i in range(shares)])
+    return whole
+
+
 def per_device(amps, six_j, interaction, deal, pandya_map, rows_live):
     groups = lax.axis_size("chan")
     _, rows, cols = amps.shape
     width = cols // groups
-    whole = lax.all_gather(interaction, "blk", axis=1, tiled=True)[0]
     outgoing = move(scatter_kernel, (cols, rows), width, pandya_map, rows_live, amps[0])
     incoming = lax.all_to_all(
         outgoing.reshape(groups, width, rows), "chan", split_axis=0, concat_axis=0, tiled=True
     )
-    six = six_j[0].reshape(groups, width, cols)[deal].reshape(cols, cols)
-    right = lax.dot_general(
-        whole, six, (((1,), (1,)), ((), ())), preferred_element_type=jnp.float32
-    ).astype(jnp.bfloat16)
-    both = lax.dot_general(
-        right, six, (((0,), (1,)), ((), ())), preferred_element_type=jnp.float32
-    ).astype(jnp.bfloat16)
+    both = chain(width, deal, six_j[0], whole_panel(interaction[0]))
     sending = jnp.dot(
         both, incoming.reshape(cols, rows), preferred_element_type=jnp.float32
     ).astype(jnp.bfloat16)

time: 91.3 us -> 71.5 us (0.78)
  between operations: 13.5 us -> 0.12 us
  matrix products: 12.6 us -> 1.24 us
  Pallas kernels: 6.45 us -> 15.2 us
  waiting for transfers between devices: 17.2 us -> 15.1 us
  local copies, waits for them, and re-layouts: 2 us -> 0.48 us
    pallas_call x0 -> x1, Pallas kernels: none -> 8.73 us  [chain(): pl.pallas_call(functools.partial(chain_kernel, width), out_shape=jax.Shap...]
    dot_general x1 -> x0, matrix products: 5.91 us -> none  [per_device(): lax.dot_general(whole, six, (((1,), (1,)), ((), ())), preferred_element_t...]
    dot_general x1, matrix products: 6.65 us -> 1.24 us  [per_device(): jnp.dot(both, incoming.reshape(cols, rows), preferred_element_type=jnp.fl...]
    all_to_all x1, waiting for transfers between devices: 15.2 us -> 12.8 us  [per_device(): lax.all_to_all(outgoing.reshape(groups, width, rows), 'chan', split_axis=...]
    ppermute x0 -> x1, waiting for transfers between devices: none -> 2.23 us  [whole_panel(): lax.ppermute(part, 'blk', [(i, (i + 1) % shares) for i in range(shares)])]
    gather x1 -> x0, local copies, waits for them, and re-layouts: 1.99 us -> none  [per_device(): six = six_j[0].reshape(groups, width, cols)[deal].reshape(cols, cols)]
    all_gather x1 -> x0, waiting for transfers between devices: 1.27 us -> none  [per_device(): whole = lax.all_gather(interaction, 'blk', axis=1, tiled=True)[0]]
  transfers between devices with their start and end apart: 2 -> 2, of which waited for: 2 -> 2; matrix products, arithmetic and copies ran while one was open for 9% -> 1% of each run, Pallas kernels for 4% -> 12%
where the time goes in v2:
time: 71.5 us; the launch traced here: 71.2 us
  blocking collectives  30.7 us (43%)
  Pallas kernels  15.2 us (21%)
  waiting for transfers between devices  15.1 us (21%)
  starting transfers between devices  8.4 us (12%)
  matrix products  1.24 us (2%)
    all_to_all x1, blocking collectives, per_device(): lax.all_to_all(sending.reshape(groups, width, rows), 'chan', split_axis=0...  30.7 us
    all_to_all x1, waiting for transfers between devices, per_device(): lax.all_to_all(outgoing.reshape(groups, width, rows), 'chan', split_axis=...  12.8 us
    pallas_call x1, Pallas kernels, chain(): pl.pallas_call(functools.partial(chain_kernel, width), out_shape=jax.Shap...  8.73 us
    all_to_all x1, starting transfers between devices, per_device(): lax.all_to_all(outgoing.reshape(groups, width, rows), 'chan', split_axis=...  8.32 us
    pallas_call x2, Pallas kernels, move(): pl.pallas_call(functools.partial(kernel, width), out_shape=jax.ShapeDtype...  6.45 us
    ppermute x1, waiting for transfers between devices, whole_panel(): lax.ppermute(part, 'blk', [(i, (i + 1) % shares) for i in range(shares)])  2.23 us
  transfers between devices with their start and end apart: 2, of which 2 were waited for; matrix products, arithmetic and copies ran while one was open for 1% of the time, Pallas kernels for 12%

profile of v2, /device:TPU:0, one launch (start us, length us, event | category | flops | bytes accessed | tf_op | source)
XLA Modules:
  0.0 71.2 jit_solution(11277926375685339056)
XLA Ops:
  0.0 0.0 copy-start.2
  0.0 3.3 %shard_map.65 = bf16[1024,512]{1,0:T(8,128)(2,1)} custom-call(s32[16]{0:T(128)} %map_ref.3, s32[16]{0:T(128)} %live_ref.3, bf16[512,1024]{1,0:T(8,128)(2,1)} %bitcast.17), custom_call_target="tpu_custom_call" | custom-call | bytes 2097152 | tf_op jit(solution)/shard_map/pallas_call | solution.py:93
  3.3 8.3 %all-to-all-start = ((bf16[16,64,512]{2,1,0:T(8,128)(2,1)}), bf16[16,64,512]{2,1,0:T(8,128)(2,1)S(1)}, u32[]{:S(2)}, u32[]{:S(2)}) async-start(bf16[16,64,512]{2,1,0:T(8,128)(2,1)} %bitcast.12), calls=%async_computation | async-start | bytes 2097152 | tf_op jit(solution)/shard_map/all_to_all | solution.py:184
  11.6 0.0 copy-done.2
  11.6 0.1 collective-permute-start
  11.7 0.3 broadcast_in_dim.6
  12.0 0.0 copy-start
  12.0 0.0 copy-start.1
  12.0 0.1 constant_dynamic-update-slice_fusion.1
  12.1 2.2 %collective-permute-done = bf16[512,1024]{1,0:T(8,128)(2,1)S(1)} collective-permute-done((bf16[512,1024]{1,0:T(8,128)(2,1)S(1)}, bf16[512,1024]{1,0:T(8,128)(2,1)S(1)}, u32[]{:S(2)}, u32[]{:S(2)}) %collective-permute-start) | collective-permute-done | bytes 1048608 | tf_op jit(solution)/shard_map/ppermute | solution.py:175
  14.4 0.1 constant_dynamic-update-slice_fusion.panel_ref
  14.5 0.0 copy-done
  14.5 0.0 copy-done.1
  14.5 8.7 %shard_map.64 = bf16[1024,1024]{1,0:T(8,128)(2,1)S(1)} custom-call(s32[16]{0:T(128)S(1)} %copy-done.1, bf16[1024,1024]{1,0:T(8,128)(2,1)S(1)} %bitcast.11, bf16[1024,1024]{1,0:T(8,128)(2,1)S(1)} %constant_dynamic-update-slice_fusion.panel_ref), custom_call_target="tpu_custom_call" | custom-call | flops 4294967296 | bytes 6291456 | tf_op jit(solution)/shard_map/pallas_call | solution.py:143
  23.2 12.8 %all-to-all-done = bf16[16,64,512]{2,1,0:T(8,128)(2,1)S(1)} async-done(((bf16[16,64,512]{2,1,0:T(8,128)(2,1)}), bf16[16,64,512]{2,1,0:T(8,128)(2,1)S(1)}, u32[]{:S(2)}, u32[]{:S(2)}) %all-to-all-start) | async-done | bytes 1048608 | tf_op jit(solution)/shard_map/all_to_all | solution.py:184
  36.1 1.2 %convolution_convert_fusion = bf16[1024,512]{1,0:T(8,128)(2,1)S(1)} fusion(bf16[1024,1024]{1,0:T(8,128)(2,1)S(1)} %shard_map.64, bf16[1024,512]{1,0:T(8,128)(2,1)S(1)} %bitcast.15), kind=kOutput, calls=%fused_computation | convolution fusion | flops 1074266112 | bytes 4194304 | tf_op jit(solution)/shard_map/dot_general | solution.py:188
  37.3 30.7 %all_to_all.10 = bf16[16,64,512]{2,1,0:T(8,128)(2,1)} all-to-all(bf16[16,64,512]{2,1,0:T(8,128)(2,1)S(1)} %bitcast.16), channel_id=1, replica_groups=mesh['chan'=16,'blk'=2] {'chan'}, dimensions={0} | all-to-all | bytes 2097152 | tf_op jit(solution)/shard_map/all_to_all | solution.py:191
  68.0 3.2 %shard_map.66 = bf16[512,1024]{1,0:T(8,128)(2,1)} custom-call(s32[16]{0:T(128)} %map_ref.3, s32[16]{0:T(128)} %live_ref.3, bf16[1024,512]{1,0:T(8,128)(2,1)} %bitcast.13), custom_call_target="tpu_custom_call" | custom-call | bytes 2097152 | tf_op jit(solution)/shard_map/pallas_call | solution.py:93
Async XLA Ops:
  0.0 11.6 %copy-start.2 = (bf16[1,512,1024]{2,1,0:T(8,128)(2,1)S(1)}, bf16[1,512,1024]{2,1,0:T(8,128)(2,1)}, u32[]{:S(2)}) copy-start(bf16[1,512,1024]{2,1,0:T(8,128)(2,1)} %param.8) | copy-start | bytes 3145732
  3.3 32.8 %all-to-all-start = ((bf16[16,64,512]{2,1,0:T(8,128)(2,1)}), bf16[16,64,512]{2,1,0:T(8,128)(2,1)S(1)}, u32[]{:S(2)}, u32[]{:S(2)}) async-start(bf16[16,64,512]{2,1,0:T(8,128)(2,1)} %bitcast.12), calls=%async_computation | async-start | bytes 2097152 | tf_op jit(solution)/shard_map/all_to_all | solution.py:184
  11.6 2.7 %collective-permute-start = (bf16[512,1024]{1,0:T(8,128)(2,1)S(1)}, bf16[512,1024]{1,0:T(8,128)(2,1)S(1)}, u32[]{:S(2)}, u32[]{:S(2)}) collective-permute-start(bf16[512,1024]{1,0:T(8,128)(2,1)S(1)} %bitcast.14), channel_id=1, source_target_pairs={{0,1},{1,0},{2,3},{3,2},{4,5},{5,4},{6,7},{7,6},{8,9},{9,8},{10,11... | collective-permute-start | bytes 3145736 | tf_op jit(solution)/shard_map/ppermute | solution.py:175
  12.0 2.5 %copy-start = (bf16[1,1024,1024]{2,1,0:T(8,128)(2,1)S(1)}, bf16[1,1024,1024]{2,1,0:T(8,128)(2,1)}, u32[]{:S(2)}) copy-start(bf16[1,1024,1024]{2,1,0:T(8,128)(2,1)} %param.7) | copy-start | bytes 6291460
  12.0 2.5 %copy-start.1 = (s32[16]{0:T(128)S(1)}, s32[16]{0:T(128)}, u32[]{:S(2)}) copy-start(s32[16]{0:T(128)} %deal_ref.1) | copy-start | bytes 196

commit v3 on v2

--- a/solution.py
+++ b/solution.py
@@ -15,31 +15,34 @@
     return ids < live
 
 
-def scatter_kernel(width, map_ref, live_ref, amps_ref, out_ref, tile, turned, in_sem, out_sem):
+def scatter_kernel(
+    width, map_ref, live_ref, amps_ref, out_ref, tile, turned, map_in, live_in, sem, out_sem, small
+):
     rows, cols = amps_ref.shape
-    slot = lax.axis_index("chan")
     first = lax.axis_index("blk") * rows
-    live = live_ref[slot]
-    tiles = cols // LANES
     per_tile = LANES // width
+    scalars = [
+        pltpu.make_async_copy(map_ref, map_in, small.at[0]),
+        pltpu.make_async_copy(live_ref, live_in, small.at[1]),
+    ]
     loads = [
-        pltpu.make_async_copy(
-            amps_ref.at[:, pl.ds(j * LANES, LANES)], tile.at[j], in_sem.at[j]
-        )
-        for j in range(tiles)
+        pltpu.make_async_copy(amps_ref.at[:, pl.ds(j * LANES, LANES)], tile.at[j], sem.at[j])
+        for j in range(cols // LANES)
     ]
-    for load in loads:
-        load.start()
-    keep = live_lanes(first, rows, live)
+    for copy in scalars + loads:
+        copy.start()
+    for copy in scalars:
+        copy.wait()
+    keep = live_lanes(first, rows, live_in[lax.axis_index("chan")])
     stores = []
-    for j in range(tiles):
-        loads[j].wait()
+    for j, load in enumerate(loads):
+        load.wait()
         turned[pl.ds(j * LANES, LANES), :] = jnp.where(keep, tile[j].T, 0)
-        for i in range(per_tile):
-            k = j * per_tile + i
+        for k in range(j * per_tile, (j + 1) * per_tile):
+            at = pl.multiple_of(map_in[k] * width, width)
             store = pltpu.make_async_copy(
                 turned.at[pl.ds(k * width, width), :],
-                out_ref.at[pl.ds(pl.multiple_of(map_ref[k] * width, width), width), :],
+                out_ref.at[pl.ds(at, width), :],
                 out_sem.at[k],
             )
             store.start()
@@ -48,31 +51,21 @@
         store.wait()
 
 
-def gather_kernel(width, map_ref, live_ref, back_ref, out_ref, turned, tile, in_sem, out_sem):
+def gather_kernel(width, map_ref, live_ref, back_ref, out_ref, tile, sem):
     rows, cols = out_ref.shape
-    slot = lax.axis_index("chan")
     first = lax.axis_index("blk") * rows
-    live = live_ref[slot]
-    tiles = cols // LANES
+    live = live_ref[lax.axis_index("chan")]
     per_tile = LANES // width
-    loads = [
-        pltpu.make_async_copy(
-            back_ref.at[pl.ds(pl.multiple_of(map_ref[k] * width, width), width), :],
-            turned.at[pl.ds(k * width, width), :],
-            in_sem.at[k],
-        )
-        for k in range(cols // width)
-    ]
-    for load in loads:
-        load.start()
     keep = live_lanes(first, rows, live)
     stores = []
-    for j in range(tiles):
+    for j in range(cols // LANES):
+        blocks = []
         for i in range(per_tile):
-            loads[j * per_tile + i].wait()
-        tile[j] = jnp.where(keep, turned[pl.ds(j * LANES, LANES), :], 0).T
+            at = pl.multiple_of(map_ref[j * per_tile + i] * width, width)
+            blocks.append(back_ref[pl.ds(at, width), :])
+        tile[j] = jnp.where(keep, jnp.concatenate(blocks, axis=0), 0).T
         store = pltpu.make_async_copy(
-            tile.at[j], out_ref.at[:, pl.ds(j * LANES, LANES)], out_sem.at[j]
+            tile.at[j], out_ref.at[:, pl.ds(j * LANES, LANES)], sem.at[j]
         )
         store.start()
         stores.append(store)
@@ -80,26 +73,45 @@
         store.wait()
 
 
-def move(kernel, out_shape, width, pandya_map, rows_live, block):
-    cols, rows = out_shape if kernel is scatter_kernel else block.shape
-    tile = pltpu.VMEM((cols // LANES, rows, LANES), jnp.bfloat16)
-    turned = pltpu.VMEM((cols, rows), jnp.bfloat16)
-    tile_sem = pltpu.SemaphoreType.DMA((cols // LANES,))
-    group_sem = pltpu.SemaphoreType.DMA((cols // width,))
-    if kernel is scatter_kernel:
-        scratch = [tile, turned, tile_sem, group_sem]
-    else:
-        scratch = [turned, tile, group_sem, tile_sem]
+def scatter(width, pandya_map, rows_live, block):
+    rows, cols = block.shape
+    count = cols // width
     return pl.pallas_call(
-        functools.partial(kernel, width),
-        out_shape=jax.ShapeDtypeStruct(out_shape, jnp.bfloat16),
+        functools.partial(scatter_kernel, width),
+        out_shape=jax.ShapeDtypeStruct((cols, rows), jnp.bfloat16),
+        in_specs=[pl.BlockSpec(memory_space=pl.ANY)] * 3,
+        out_specs=pl.BlockSpec(memory_space=pl.ANY),
+        scratch_shapes=[
+            pltpu.VMEM((cols // LANES, rows, LANES), jnp.bfloat16),
+            pltpu.VMEM((cols, rows), jnp.bfloat16),
+            pltpu.SMEM((count,), jnp.int32),
+            pltpu.SMEM((count,), jnp.int32),
+            pltpu.SemaphoreType.DMA((cols // LANES,)),
+            pltpu.SemaphoreType.DMA((count,)),
+            pltpu.SemaphoreType.DMA((2,)),
+        ],
+        cost_estimate=pl.CostEstimate(
+            flops=0, bytes_accessed=4 * cols * rows, transcendentals=0
+        ),
+    )(pandya_map, rows_live, block)
+
+
+def gather(width, pandya_map, rows_live, block):
+    cols, rows = block.shape
+    return pl.pallas_call(
+        functools.partial(gather_kernel, width),
+        out_shape=jax.ShapeDtypeStruct((rows, cols), jnp.bfloat16),
         in_specs=[
             pl.BlockSpec(memory_space=pltpu.SMEM),
             pl.BlockSpec(memory_space=pltpu.SMEM),
-            pl.BlockSpec(memory_space=pl.ANY),
+            pl.BlockSpec(memory_space=pltpu.VMEM),
         ],
         out_specs=pl.BlockSpec(memory_space=pl.ANY),
-        scratch_shapes=scratch,
+        scratch_shapes=[
+            pltpu.VMEM((cols // LANES, rows, LANES), jnp.bfloat16),
+            pltpu.SemaphoreType.DMA((cols // LANES,)),
+        ],
+        compiler_params=pltpu.CompilerParams(vmem_limit_bytes=8 * 1024 * 1024),
         cost_estimate=pl.CostEstimate(
             flops=0, bytes_accessed=4 * cols * rows, transcendentals=0
         ),
@@ -180,7 +192,7 @@
     groups = lax.axis_size("chan")
     _, rows, cols = amps.shape
     width = cols // groups
-    outgoing = move(scatter_kernel, (cols, rows), width, pandya_map, rows_live, amps[0])
+    outgoing = scatter(width, pandya_map, rows_live, amps[0])
     incoming = lax.all_to_all(
         outgoing.reshape(groups, width, rows), "chan", split_axis=0, concat_axis=0, tiled=True
     )
@@ -191,9 +203,7 @@
     arriving = lax.all_to_all(
         sending.reshape(groups, width, rows), "chan", split_axis=0, concat_axis=0, tiled=True
     )
-    result = move(
-        gather_kernel, (rows, cols), width, pandya_map, rows_live, arriving.reshape(cols, rows)
-    )
+    result = gather(width, pandya_map, rows_live, arriving.reshape(cols, rows))
     return result[None]
 
 

time: 71.5 us -> 69.2 us (0.968)
  Pallas kernels: 15.2 us -> 13 us
    pallas_call x2, Pallas kernels: 6.45 us -> 4.27 us  [the longest x1 2.59 us: scatter(): pl.pallas_call(functools.partial(scatter_kernel, width), out_shape=jax.Sh...]
  transfers between devices with their start and end apart: 2 -> 2, of which waited for: 2 -> 2; matrix products, arithmetic and copies ran while one was open for 1% -> 1% of each run, Pallas kernels for 12% -> 13%
where the time goes in v3:
time: 69.2 us; the launch traced here: 68.9 us
  blocking collectives  30.6 us (44%)
  waiting for transfers between devices  15.1 us (22%)
  Pallas kernels  13 us (19%)
  starting transfers between devices  8.4 us (12%)
  matrix products  1.24 us (2%)
    all_to_all x1, blocking collectives, per_device(): lax.all_to_all(sending.reshape(groups, width, rows), 'chan', split_axis=0...  30.6 us
    all_to_all x1, waiting for transfers between devices, per_device(): lax.all_to_all(outgoing.reshape(groups, width, rows), 'chan', split_axis=...  12.8 us
    pallas_call x1, Pallas kernels, chain(): pl.pallas_call(functools.partial(chain_kernel, width), out_shape=jax.Shap...  8.73 us
    all_to_all x1, starting transfers between devices, per_device(): lax.all_to_all(outgoing.reshape(groups, width, rows), 'chan', split_axis=...  8.32 us
    pallas_call x1, Pallas kernels, scatter(): pl.pallas_call(functools.partial(scatter_kernel, width), out_shape=jax.Sh...  2.59 us
    ppermute x1, waiting for transfers between devices, whole_panel(): lax.ppermute(part, 'blk', [(i, (i + 1) % shares) for i in range(shares)])  2.23 us
    pallas_call x1, Pallas kernels, gather(): pl.pallas_call(functools.partial(gather_kernel, width), out_shape=jax.Sha...  1.67 us
  transfers between devices with their start and end apart: 2, of which 2 were waited for; matrix products, arithmetic and copies ran while one was open for 1% of the time, Pallas kernels for 13%

profile of v3, /device:TPU:0, one launch (start us, length us, event | category | flops | bytes accessed | tf_op | source)
XLA Modules:
  0.0 68.9 jit_solution(6601798593638346270)
XLA Ops:
  0.0 0.0 copy-start.4
  0.0 2.6 %shard_map.65 = bf16[1024,512]{1,0:T(8,128)(2,1)} custom-call(s32[16]{0:T(128)} %map_ref.3, s32[16]{0:T(128)} %live_ref.3, bf16[512,1024]{1,0:T(8,128)(2,1)} %bitcast.17), custom_call_target="tpu_custom_call" | custom-call | bytes 2097152 | tf_op jit(solution)/shard_map/pallas_call | solution.py:79
  2.6 8.3 %all-to-all-start = ((bf16[16,64,512]{2,1,0:T(8,128)(2,1)}), bf16[16,64,512]{2,1,0:T(8,128)(2,1)S(1)}, u32[]{:S(2)}, u32[]{:S(2)}) async-start(bf16[16,64,512]{2,1,0:T(8,128)(2,1)} %bitcast.13), calls=%async_computation | async-start | bytes 2097152 | tf_op jit(solution)/shard_map/all_to_all | solution.py:196
  10.9 0.0 copy-done.4
  10.9 0.1 collective-permute-start
  11.0 0.3 broadcast_in_dim.6
  11.3 0.0 copy-start.2
  11.3 0.0 copy-start.3
  11.3 0.1 constant_dynamic-update-slice_fusion.1
  11.4 2.2 %collective-permute-done = bf16[512,1024]{1,0:T(8,128)(2,1)S(1)} collective-permute-done((bf16[512,1024]{1,0:T(8,128)(2,1)S(1)}, bf16[512,1024]{1,0:T(8,128)(2,1)S(1)}, u32[]{:S(2)}, u32[]{:S(2)}) %collective-permute-start) | collective-permute-done | bytes 1048608 | tf_op jit(solution)/shard_map/ppermute | solution.py:187
  13.7 0.1 constant_dynamic-update-slice_fusion.panel_ref
  13.8 0.0 copy-done.2
  13.8 0.0 copy-done.3
  13.8 8.7 %shard_map.64 = bf16[1024,1024]{1,0:T(8,128)(2,1)S(1)} custom-call(s32[16]{0:T(128)S(1)} %copy-done.3, bf16[1024,1024]{1,0:T(8,128)(2,1)S(1)} %bitcast.12, bf16[1024,1024]{1,0:T(8,128)(2,1)S(1)} %constant_dynamic-update-slice_fusion.panel_ref), custom_call_target="tpu_custom_call" | custom-call | flops 4294967296 | bytes 6291456 | tf_op jit(solution)/shard_map/pallas_call | solution.py:155
  22.5 12.8 %all-to-all-done = bf16[16,64,512]{2,1,0:T(8,128)(2,1)S(1)} async-done(((bf16[16,64,512]{2,1,0:T(8,128)(2,1)}), bf16[16,64,512]{2,1,0:T(8,128)(2,1)S(1)}, u32[]{:S(2)}, u32[]{:S(2)}) %all-to-all-start) | async-done | bytes 1048608 | tf_op jit(solution)/shard_map/all_to_all | solution.py:196
  35.4 1.2 %convolution_convert_fusion = bf16[1024,512]{1,0:T(8,128)(2,1)S(1)} fusion(bf16[1024,1024]{1,0:T(8,128)(2,1)S(1)} %shard_map.64, bf16[1024,512]{1,0:T(8,128)(2,1)S(1)} %bitcast.15), kind=kOutput, calls=%fused_computation | convolution fusion | flops 1074266112 | bytes 4194304 | tf_op jit(solution)/shard_map/dot_general | solution.py:200
  36.6 0.0 copy-start
  36.6 0.0 copy-start.1
  36.7 30.6 %all_to_all.10 = bf16[16,64,512]{2,1,0:T(8,128)(2,1)S(1)} all-to-all(bf16[16,64,512]{2,1,0:T(8,128)(2,1)S(1)} %bitcast.16), channel_id=1, replica_groups=mesh['chan'=16,'blk'=2] {'chan'}, dimensions={0} | all-to-all | bytes 2097152 | tf_op jit(solution)/shard_map/all_to_all | solution.py:203
  67.2 0.0 copy-done
  67.2 0.0 copy-done.1
  67.2 1.7 %shard_map.66 = bf16[512,1024]{1,0:T(8,128)(2,1)} custom-call(s32[16]{0:T(128)S(1)} %copy-done, s32[16]{0:T(128)S(1)} %copy-done.1, bf16[1024,512]{1,0:T(8,128)(2,1)S(1)} %bitcast.11), custom_call_target="tpu_custom_call" | custom-call | bytes 2097152 | tf_op jit(solution)/shard_map/pallas_call | solution.py:101
Async XLA Ops:
  0.0 10.9 %copy-start.4 = (bf16[1,512,1024]{2,1,0:T(8,128)(2,1)S(1)}, bf16[1,512,1024]{2,1,0:T(8,128)(2,1)}, u32[]{:S(2)}) copy-start(bf16[1,512,1024]{2,1,0:T(8,128)(2,1)} %param.8) | copy-start | bytes 3145732
  2.6 32.8 %all-to-all-start = ((bf16[16,64,512]{2,1,0:T(8,128)(2,1)}), bf16[16,64,512]{2,1,0:T(8,128)(2,1)S(1)}, u32[]{:S(2)}, u32[]{:S(2)}) async-start(bf16[16,64,512]{2,1,0:T(8,128)(2,1)} %bitcast.13), calls=%async_computation | async-start | bytes 2097152 | tf_op jit(solution)/shard_map/all_to_all | solution.py:196
  10.9 2.7 %collective-permute-start = (bf16[512,1024]{1,0:T(8,128)(2,1)S(1)}, bf16[512,1024]{1,0:T(8,128)(2,1)S(1)}, u32[]{:S(2)}, u32[]{:S(2)}) collective-permute-start(bf16[512,1024]{1,0:T(8,128)(2,1)S(1)} %bitcast.14), channel_id=1, source_target_pairs={{0,1},{1,0},{2,3},{3,2},{4,5},{5,4},{6,7},{7,6},{8,9},{9,8},{10,11... | collective-permute-start | bytes 3145736 | tf_op jit(solution)/shard_map/ppermute | solution.py:187
  11.3 2.5 %copy-start.2 = (bf16[1,1024,1024]{2,1,0:T(8,128)(2,1)S(1)}, bf16[1,1024,1024]{2,1,0:T(8,128)(2,1)}, u32[]{:S(2)}) copy-start(bf16[1,1024,1024]{2,1,0:T(8,128)(2,1)} %param.7) | copy-start | bytes 6291460
  11.3 2.5 %copy-start.3 = (s32[16]{0:T(128)S(1)}, s32[16]{0:T(128)}, u32[]{:S(2)}) copy-start(s32[16]{0:T(128)} %deal_ref.1) | copy-start | bytes 196
  36.6 30.6 %copy-start = (s32[16]{0:T(128)S(1)}, s32[16]{0:T(128)}, u32[]{:S(2)}) copy-start(s32[16]{0:T(128)} %map_ref.3) | copy-start | bytes 196
  36.6 30.6 %copy-start.1 = (s32[16]{0:T(128)S(1)}, s32[16]{0:T(128)}, u32[]{:S(2)}) copy-start(s32[16]{0:T(128)} %live_ref.3) | copy-start | bytes 196

commit v4 on v3

--- a/solution.py
+++ b/solution.py
@@ -8,6 +8,7 @@
 from jax.sharding import PartitionSpec as P
 
 LANES = 128
+FIRST_TURN = 0
 
 
 def live_lanes(first, rows, live):
@@ -118,85 +119,129 @@
     )(pandya_map, rows_live, block)
 
 
-def chain_kernel(width, deal_ref, six_ref, panel_ref, out_ref, six, panel, right, six_sem, panel_sem):
+def chain_kernel(width, turn, shares, *refs):
+    deal_ref, six_ref = refs[:2]
+    part_refs = refs[2 : 2 + shares]
+    out_ref, six, panel, result, deal, deal_sem, six_sem, panel_sem, out_sem = refs[-9:]
     cols = six.shape[0]
-    fetch = [
-        pltpu.make_async_copy(
-            six_ref.at[pl.ds(pl.multiple_of(deal_ref[s] * width, width), width), :],
-            six.at[pl.ds(s * width, width), :],
-            six_sem.at[s],
-        )
-        for s in range(cols // width)
-    ]
-    fetch_panel = pltpu.make_async_copy(panel_ref, panel, panel_sem)
-    fetch_panel.start()
-    for copy in fetch:
-        copy.start()
-    for copy in fetch:
-        copy.wait()
-    fetch_panel.wait()
+    rows = cols // shares
     step = min(256, cols)
-    across = (((1,), (1,)), ((), ()))
-
-    @pl.loop(0, cols // step)
-    def _(i):
-        at = pl.ds(pl.multiple_of(i * step, step), step)
-        right[at, :] = lax.dot_general(
-            six[at, :], panel[...], across, preferred_element_type=jnp.float32
-        ).astype(jnp.bfloat16)
-        out_ref[at, :] = lax.dot_general(
-            right[at, :], six[...], across, preferred_element_type=jnp.float32
-        ).astype(jnp.bfloat16)
-
-
-def chain(width, deal, six, panel):
+    me = lax.axis_index("blk")
+    mine = lax.rem(me, 2) == turn
+
+    @pl.when(mine)
+    def _():
+        fetch_deal = pltpu.make_async_copy(deal_ref, deal, deal_sem)
+        fetch_deal.start()
+        parts = []
+        for i, part_ref in enumerate(part_refs):
+            owner = lax.rem(me + shares - i, shares)
+            at = pl.ds(pl.multiple_of(owner * rows, rows), rows)
+            parts.append(pltpu.make_async_copy(part_ref, panel.at[at, :], panel_sem.at[i]))
+        for copy in parts:
+            copy.start()
+        fetch_deal.wait()
+        blocks = [
+            pltpu.make_async_copy(
+                six_ref.at[pl.ds(pl.multiple_of(deal[s] * width, width), width), :],
+                six.at[pl.ds(s * width, width), :],
+                six_sem.at[s],
+            )
+            for s in range(cols // width)
+        ]
+        for copy in blocks:
+            copy.start()
+        for copy in blocks + parts:
+            copy.wait()
+        across = (((1,), (1,)), ((), ()))
+        stores = []
+        for i in range(cols // step):
+            at = pl.ds(i * step, step)
+            right = lax.dot_general(
+                six[at, :], panel[...], across, preferred_element_type=jnp.float32
+            )
+            high = right.astype(jnp.bfloat16)
+            low = (right - high.astype(jnp.float32)).astype(jnp.bfloat16)
+            total = lax.dot_general(high, six[...], across, preferred_element_type=jnp.float32)
+            total += lax.dot_general(low, six[...], across, preferred_element_type=jnp.float32)
+            result[at, :] = total.astype(jnp.bfloat16)
+            store = pltpu.make_async_copy(result.at[at, :], out_ref.at[at, :], out_sem.at[i])
+            store.start()
+            stores.append(store)
+        for store in stores:
+            store.wait()
+
+
+def chain(width, turn, deal, six, parts, before=()):
     cols = six.shape[0]
-    square = pltpu.VMEM((cols, cols), jnp.bfloat16)
-    return pl.pallas_call(
-        functools.partial(chain_kernel, width),
+    shares = len(parts)
+    step = min(256, cols)
+    any_space = pl.BlockSpec(memory_space=pl.ANY)
+    scratch = pltpu.VMEM((cols, cols), jnp.bfloat16)
+    return pl.pallas_call(
+        functools.partial(chain_kernel, width, turn, shares),
         out_shape=jax.ShapeDtypeStruct((cols, cols), jnp.bfloat16),
-        in_specs=[
-            pl.BlockSpec(memory_space=pltpu.SMEM),
-            pl.BlockSpec(memory_space=pl.ANY),
-            pl.BlockSpec(memory_space=pl.ANY),
-        ],
+        in_specs=[any_space] * (2 + shares + len(before)),
+        out_specs=any_space,
+        input_output_aliases={2 + shares: 0} if before else {},
+        scratch_shapes=[
+            scratch,
+            scratch,
+            scratch,
+            pltpu.SMEM((cols // width,), jnp.int32),
+            pltpu.SemaphoreType.DMA,
+            pltpu.SemaphoreType.DMA((cols // width,)),
+            pltpu.SemaphoreType.DMA((shares,)),
+            pltpu.SemaphoreType.DMA((cols // step,)),
+        ],
+        cost_estimate=pl.CostEstimate(
+            flops=6 * cols**3, bytes_accessed=6 * cols * cols, transcendentals=0
+        ),
+    )(deal, six, *parts, *before)
+
+
+def near_kernel(far_ref, near_ref, sem):
+    copy = pltpu.make_async_copy(far_ref, near_ref, sem)
+    copy.start()
+    copy.wait()
+
+
+def near(block):
+    return pl.pallas_call(
+        near_kernel,
+        out_shape=jax.ShapeDtypeStruct(block.shape, block.dtype),
+        in_specs=[pl.BlockSpec(memory_space=pl.ANY)],
         out_specs=pl.BlockSpec(memory_space=pltpu.VMEM),
-        scratch_shapes=[
-            square,
-            square,
-            square,
-            pltpu.SemaphoreType.DMA((cols // width,)),
-            pltpu.SemaphoreType.DMA,
-        ],
-        compiler_params=pltpu.CompilerParams(vmem_limit_bytes=24 * 1024 * 1024),
-        cost_estimate=pl.CostEstimate(
-            flops=4 * cols**3, bytes_accessed=6 * cols * cols, transcendentals=0
-        ),
-    )(deal, six, panel)
-
-
-def whole_panel(part):
+        scratch_shapes=[pltpu.SemaphoreType.DMA],
+        compiler_params=pltpu.CompilerParams(vmem_limit_bytes=4 * 1024 * 1024),
+        cost_estimate=pl.CostEstimate(
+            flops=0, bytes_accessed=4 * block.size, transcendentals=0
+        ),
+    )(block)
+
+
+def panel_parts(part):
     shares = lax.axis_size("blk")
-    me = lax.axis_index("blk")
-    rows, cols = part.shape
-    whole = jnp.zeros((shares * rows, cols), part.dtype)
-    for step in range(shares):
-        owner = lax.rem(me + shares - step, shares)
-        whole = lax.dynamic_update_slice(whole, part, (owner * rows, 0))
-        if step < shares - 1:
-            part = lax.ppermute(part, "blk", [(i, (i + 1) % shares) for i in range(shares)])
-    return whole
+    parts = [part]
+    for _ in range(shares - 1):
+        part = lax.ppermute(part, "blk", [(i, (i + 1) % shares) for i in range(shares)])
+        parts.append(part)
+    return parts
 
 
 def per_device(amps, six_j, interaction, deal, pandya_map, rows_live):
     groups = lax.axis_size("chan")
     _, rows, cols = amps.shape
     width = cols // groups
+    parts = panel_parts(interaction[0])
     outgoing = scatter(width, pandya_map, rows_live, amps[0])
+    both = chain(width, FIRST_TURN, deal, six_j[0], parts)
+    outgoing, both = lax.optimization_barrier((outgoing, both))
     incoming = lax.all_to_all(
         outgoing.reshape(groups, width, rows), "chan", split_axis=0, concat_axis=0, tiled=True
     )
-    both = chain(width, deal, six_j[0], whole_panel(interaction[0]))
+    both = chain(width, 1 - FIRST_TURN, deal, six_j[0], parts, (both,))
+    both = near(both)
     sending = jnp.dot(
         both, incoming.reshape(cols, rows), preferred_element_type=jnp.float32
     ).astype(jnp.bfloat16)

time: 69.2 us -> 65.6 us (0.948)
  blocking collectives: 30.6 us -> 24 us
  local copies, waits for them, and re-layouts: 0.5 us -> 2.56 us
  Pallas kernels: 13 us -> 14.8 us
  waiting for transfers between devices: 15.1 us -> 13.8 us
    all_to_all x1, blocking collectives: 30.6 us -> 24 us  [per_device(): lax.all_to_all(sending.reshape(groups, width, rows), 'chan', split_axis=0...]
    unnamed x10 -> x8, local copies, waits for them, and re-layouts: 0.03 us -> 2.56 us
    ppermute x1, waiting for transfers between devices: 2.23 us -> 0.01 us  [panel_parts(): lax.ppermute(part, 'blk', [(i, (i + 1) % shares) for i in range(shares)])]
    pallas_call x1 -> x3, Pallas kernels: 8.73 us -> 10.6 us  [the longest x2 10.4 us: chain(): pl.pallas_call(functools.partial(chain_kernel, width, turn, shares), out_...]
    all_to_all x1, waiting for transfers between devices: 12.8 us -> 13.8 us  [per_device(): lax.all_to_all(outgoing.reshape(groups, width, rows), 'chan', split_axis=...]
  transfers between devices with their start and end apart: 2 -> 2, of which waited for: 2 -> 1; matrix products, arithmetic and copies ran while one was open for 1% -> 0% of each run, Pallas kernels for 13% -> 5%
where the time goes in v4:
time: 65.6 us; the launch traced here: 65.3 us
  blocking collectives  24 us (37%)
  Pallas kernels  14.8 us (23%)
  waiting for transfers between devices  13.8 us (21%)
  starting transfers between devices  8.67 us (13%)
  local copies, waits for them, and re-layouts  2.56 us (4%)
  matrix products  1.24 us (2%)
    all_to_all x1, blocking collectives, per_device(): lax.all_to_all(sending.reshape(groups, width, rows), 'chan', split_axis=0...  24 us
    all_to_all x1, waiting for transfers between devices, per_device(): lax.all_to_all(outgoing.reshape(groups, width, rows), 'chan', split_axis=...  13.8 us
    pallas_call x2, Pallas kernels, chain(): pl.pallas_call(functools.partial(chain_kernel, width, turn, shares), out_...  10.4 us
    all_to_all x1, starting transfers between devices, per_device(): lax.all_to_all(outgoing.reshape(groups, width, rows), 'chan', split_axis=...  8.22 us
    unnamed x8, local copies, waits for them, and re-layouts  2.56 us
    pallas_call x1, Pallas kernels, scatter(): pl.pallas_call(functools.partial(scatter_kernel, width), out_shape=jax.Sh...  2.5 us
    pallas_call x1, Pallas kernels, gather(): pl.pallas_call(functools.partial(gather_kernel, width), out_shape=jax.Sha...  1.67 us
  transfers between devices with their start and end apart: 2, of which 1 were waited for; matrix products, arithmetic and copies ran while one was open for 0% of the time, Pallas kernels for 5%

profile of v4, /device:TPU:0, one launch (start us, length us, event | category | flops | bytes accessed | tf_op | source)
XLA Modules:
  0.0 65.3 jit_solution(1238219409009276297)
XLA Ops:
  0.0 0.5 collective-permute-start
  0.5 2.5 %shard_map.64 = bf16[1024,512]{1,0:T(8,128)(2,1)} custom-call(s32[16]{0:T(128)} %map_ref.3, s32[16]{0:T(128)} %live_ref.3, bf16[512,1024]{1,0:T(8,128)(2,1)} %bitcast.13), custom_call_target="tpu_custom_call" | custom-call | bytes 2097152 | tf_op jit(solution)/shard_map/pallas_call | solution.py:80
  3.0 0.0 collective-permute-done.refs_3_
  3.0 0.0 copy-start.3
  3.0 1.0 %copy-done.3 = bf16[512,1024]{1,0:T(8,128)(2,1)} copy-done((bf16[512,1024]{1,0:T(8,128)(2,1)}, bf16[512,1024]{1,0:T(8,128)(2,1)S(1)}, u32[]{:S(2)}) %copy-start.3) | copy-done | bytes 1048600
  3.9 10.0 %shard_map.65.refs_4_ = bf16[1024,1024]{1,0:T(8,128)(2,1)} custom-call(s32[16]{0:T(128)} %refs_0_.3, bf16[1024,1024]{1,0:T(8,128)(2,1)} %bitcast.14, bf16[512,1024]{1,0:T(8,128)(2,1)} %bitcast.17, bf16[512,1024]{1,0:T(8,128)(2,1)} %copy-done.3), custom_call_target="tpu_custom_call" | custom-call | flops 6442450944 | bytes 6291456 | tf_op jit(solution)/shard_map/pallas_call | solution.py:181
  14.0 8.2 %all-to-all-start = ((bf16[16,64,512]{2,1,0:T(8,128)(2,1)}), bf16[16,64,512]{2,1,0:T(8,128)(2,1)S(1)}, u32[]{:S(2)}, u32[]{:S(2)}) async-start(bf16[16,64,512]{2,1,0:T(8,128)(2,1)} %bitcast.3), calls=%async_computation | async-start | bytes 2097152 | tf_op jit(solution)/shard_map/all_to_all | solution.py:240
  22.2 0.4 shard_map.66.far_ref
  22.6 0.0 copy-start
  22.6 1.6 %copy-done = bf16[1024,1024]{1,0:T(8,128)(2,1)S(1)} copy-done((bf16[1024,1024]{1,0:T(8,128)(2,1)S(1)}, bf16[1024,1024]{1,0:T(8,128)(2,1)}, u32[]{:S(2)}) %copy-start) | copy-done | bytes 2097176
  24.2 0.1 shard_map.67
  24.4 13.8 %all-to-all-done = bf16[16,64,512]{2,1,0:T(8,128)(2,1)S(1)} async-done(((bf16[16,64,512]{2,1,0:T(8,128)(2,1)}), bf16[16,64,512]{2,1,0:T(8,128)(2,1)S(1)}, u32[]{:S(2)}, u32[]{:S(2)}) %all-to-all-start) | async-done | bytes 1048608 | tf_op jit(solution)/shard_map/all_to_all | solution.py:240
  38.2 1.2 %convolution_convert_fusion = bf16[1024,512]{1,0:T(8,128)(2,1)S(1)} fusion(bf16[1024,1024]{1,0:T(8,128)(2,1)S(1)} %shard_map.67, bf16[1024,512]{1,0:T(8,128)(2,1)S(1)} %bitcast.11), kind=kOutput, calls=%fused_computation | convolution fusion | flops 1074266112 | bytes 4194304 | tf_op jit(solution)/shard_map/dot_general | solution.py:245
  39.4 0.0 copy-start.1
  39.4 0.0 copy-start.2
  39.5 24.0 %all_to_all.10 = bf16[16,64,512]{2,1,0:T(8,128)(2,1)S(1)} all-to-all(bf16[16,64,512]{2,1,0:T(8,128)(2,1)S(1)} %bitcast.12), channel_id=1, replica_groups=mesh['chan'=16,'blk'=2] {'chan'}, dimensions={0} | all-to-all | bytes 2097152 | tf_op jit(solution)/shard_map/all_to_all | solution.py:248
  63.4 0.0 copy-done.1
  63.5 0.0 copy-done.2
  63.5 1.7 %shard_map.68 = bf16[512,1024]{1,0:T(8,128)(2,1)} custom-call(s32[16]{0:T(128)S(1)} %copy-done.1, s32[16]{0:T(128)S(1)} %copy-done.2, bf16[1024,512]{1,0:T(8,128)(2,1)S(1)} %bitcast.10), custom_call_target="tpu_custom_call" | custom-call | bytes 2097152 | tf_op jit(solution)/shard_map/pallas_call | solution.py:102
Async XLA Ops:
  0.0 3.0 %collective-permute-start = (bf16[512,1024]{1,0:T(8,128)(2,1)}, bf16[512,1024]{1,0:T(8,128)(2,1)S(1)}, u32[]{:S(2)}, u32[]{:S(2)}) collective-permute-start(bf16[512,1024]{1,0:T(8,128)(2,1)} %bitcast.16), channel_id=1, source_target_pairs={{0,1},{1,0},{2,3},{3,2},{4,5},{5,4},{6,7},{7,6},{8,9},{9,8},{10,11... | collective-permute-start | bytes 3145736 | tf_op jit(solution)/shard_map/ppermute | solution.py:227
  3.0 1.0 %copy-start.3 = (bf16[512,1024]{1,0:T(8,128)(2,1)}, bf16[512,1024]{1,0:T(8,128)(2,1)S(1)}, u32[]{:S(2)}) copy-start(bf16[512,1024]{1,0:T(8,128)(2,1)S(1)} %collective-permute-done.refs_3_) | copy-start | bytes 3145732
  14.0 24.2 %all-to-all-start = ((bf16[16,64,512]{2,1,0:T(8,128)(2,1)}), bf16[16,64,512]{2,1,0:T(8,128)(2,1)S(1)}, u32[]{:S(2)}, u32[]{:S(2)}) async-start(bf16[16,64,512]{2,1,0:T(8,128)(2,1)} %bitcast.3), calls=%async_computation | async-start | bytes 2097152 | tf_op jit(solution)/shard_map/all_to_all | solution.py:240
  22.6 1.6 %copy-start = (bf16[1024,1024]{1,0:T(8,128)(2,1)S(1)}, bf16[1024,1024]{1,0:T(8,128)(2,1)}, u32[]{:S(2)}) copy-start(bf16[1024,1024]{1,0:T(8,128)(2,1)} %shard_map.66.far_ref) | copy-start | bytes 6291460
  39.4 24.0 %copy-start.1 = (s32[16]{0:T(128)S(1)}, s32[16]{0:T(128)}, u32[]{:S(2)}) copy-start(s32[16]{0:T(128)} %map_ref.3) | copy-start | bytes 196
  39.4 24.0 %copy-start.2 = (s32[16]{0:T(128)S(1)}, s32[16]{0:T(128)}, u32[]{:S(2)}) copy-start(s32[16]{0:T(128)} %live_ref.3) | copy-start | bytes 196

commit v5 on v4

--- a/solution.py
+++ b/solution.py
@@ -8,7 +8,8 @@
 from jax.sharding import PartitionSpec as P
 
 LANES = 128
-FIRST_TURN = 0
+AHEAD = 0
+TERMS = 3
 
 
 def live_lanes(first, rows, live):
@@ -119,85 +120,170 @@
     )(pandya_map, rows_live, block)
 
 
-def chain_kernel(width, turn, shares, *refs):
+def add_part(six, at, part, across_at, total, terms):
+    across = (((1,), (1,)), ((), ()))
+    rest = lax.dot_general(six[at, :], part, across, preferred_element_type=jnp.float32)
+    for _ in range(terms):
+        term = rest.astype(jnp.bfloat16)
+        rest = rest - term.astype(jnp.float32)
+        share = lax.dot_general(
+            term, six[:, across_at], across, preferred_element_type=jnp.float32
+        )
+        total = share if total is None else total + share
+    return total
+
+
+def fetch_six(width, deal_ref, six_ref, deal, six, deal_sem, six_sem):
+    fetch_deal = pltpu.make_async_copy(deal_ref, deal, deal_sem)
+    fetch_deal.start()
+    fetch_deal.wait()
+    blocks = [
+        pltpu.make_async_copy(
+            six_ref.at[pl.ds(pl.multiple_of(deal[s] * width, width), width), :],
+            six.at[pl.ds(s * width, width), :],
+            six_sem.at[s],
+        )
+        for s in range(six.shape[0] // width)
+    ]
+    for copy in blocks:
+        copy.start()
+    return blocks
+
+
+def owner_range(i, shares, rows):
+    owner = lax.rem(lax.axis_index("blk") + shares - i, shares)
+    return pl.ds(pl.multiple_of(owner * rows, rows), rows)
+
+
+def ahead_tiles(cols):
+    step = min(256, cols)
+    starts = [0, step // 2] + list(range(step, cols, step))
+    return [(a, b - a) for a, b in zip(starts, starts[1:] + [cols])]
+
+
+def ahead_kernel(
+    width, shares, deal_ref, six_ref, part_ref, sum_ref, six, part, total, deal, deal_sem, six_sem, part_sem, out_sem
+):
+    cols = six.shape[0]
+    tiles = ahead_tiles(cols)
+
+    @pl.when(lax.rem(lax.axis_index("blk"), 2) == AHEAD)
+    def _():
+        fetch_part = pltpu.make_async_copy(part_ref, part, part_sem)
+        fetch_part.start()
+        for copy in fetch_six(width, deal_ref, six_ref, deal, six, deal_sem, six_sem):
+            copy.wait()
+        fetch_part.wait()
+        stores = []
+        for i, (start, size) in enumerate(tiles):
+            at = pl.ds(start, size)
+            total[at, :] = add_part(
+                six, at, part[...], owner_range(0, shares, part.shape[0]), None, TERMS
+            )
+            store = pltpu.make_async_copy(total.at[at, :], sum_ref.at[at, :], out_sem.at[i])
+            store.start()
+            stores.append(store)
+        for store in stores:
+            store.wait()
+
+
+def ahead(width, shares, deal, six, part):
+    cols = six.shape[0]
+    any_space = pl.BlockSpec(memory_space=pl.ANY)
+    return pl.pallas_call(
+        functools.partial(ahead_kernel, width, shares),
+        out_shape=jax.ShapeDtypeStruct((cols, cols), jnp.float32),
+        in_specs=[any_space] * 3,
+        out_specs=any_space,
+        scratch_shapes=[
+            pltpu.VMEM((cols, cols), jnp.bfloat16),
+            pltpu.VMEM(part.shape, jnp.bfloat16),
+            pltpu.VMEM((cols, cols), jnp.float32),
+            pltpu.SMEM((cols // width,), jnp.int32),
+            pltpu.SemaphoreType.DMA,
+            pltpu.SemaphoreType.DMA((cols // width,)),
+            pltpu.SemaphoreType.DMA,
+            pltpu.SemaphoreType.DMA((len(ahead_tiles(cols)),)),
+        ],
+        cost_estimate=pl.CostEstimate(
+            flops=2 * cols**3, bytes_accessed=8 * cols * cols, transcendentals=0
+        ),
+    )(deal, six, part)
+
+
+def chain_kernel(width, shares, *refs):
     deal_ref, six_ref = refs[:2]
     part_refs = refs[2 : 2 + shares]
-    out_ref, six, panel, result, deal, deal_sem, six_sem, panel_sem, out_sem = refs[-9:]
+    sum_ref, out_ref, six, part, total, result, deal, deal_sem, six_sem, part_sem, sum_sem, out_sem = (
+        refs[2 + shares :]
+    )
     cols = six.shape[0]
+    step = min(256, cols)
     rows = cols // shares
-    step = min(256, cols)
-    me = lax.axis_index("blk")
-    mine = lax.rem(me, 2) == turn
-
-    @pl.when(mine)
-    def _():
-        fetch_deal = pltpu.make_async_copy(deal_ref, deal, deal_sem)
-        fetch_deal.start()
-        parts = []
-        for i, part_ref in enumerate(part_refs):
-            owner = lax.rem(me + shares - i, shares)
-            at = pl.ds(pl.multiple_of(owner * rows, rows), rows)
-            parts.append(pltpu.make_async_copy(part_ref, panel.at[at, :], panel_sem.at[i]))
+    was_ahead = lax.rem(lax.axis_index("blk"), 2) == AHEAD
+
+    def form(first):
+        if first:
+            fetch_sum = pltpu.make_async_copy(sum_ref, total, sum_sem)
+            fetch_sum.start()
+        parts = [
+            pltpu.make_async_copy(part_refs[i], part.at[i], part_sem.at[i])
+            for i in range(first, shares)
+        ]
         for copy in parts:
             copy.start()
-        fetch_deal.wait()
-        blocks = [
-            pltpu.make_async_copy(
-                six_ref.at[pl.ds(pl.multiple_of(deal[s] * width, width), width), :],
-                six.at[pl.ds(s * width, width), :],
-                six_sem.at[s],
-            )
-            for s in range(cols // width)
-        ]
-        for copy in blocks:
-            copy.start()
+        blocks = fetch_six(width, deal_ref, six_ref, deal, six, deal_sem, six_sem)
         for copy in blocks + parts:
             copy.wait()
-        across = (((1,), (1,)), ((), ()))
+        if first:
+            fetch_sum.wait()
         stores = []
         for i in range(cols // step):
             at = pl.ds(i * step, step)
-            right = lax.dot_general(
-                six[at, :], panel[...], across, preferred_element_type=jnp.float32
-            )
-            high = right.astype(jnp.bfloat16)
-            low = (right - high.astype(jnp.float32)).astype(jnp.bfloat16)
-            total = lax.dot_general(high, six[...], across, preferred_element_type=jnp.float32)
-            total += lax.dot_general(low, six[...], across, preferred_element_type=jnp.float32)
-            result[at, :] = total.astype(jnp.bfloat16)
+            value = total[at, :] if first else None
+            for p in range(first, shares):
+                value = add_part(six, at, part[p], owner_range(p, shares, rows), value, TERMS)
+            result[at, :] = value.astype(jnp.bfloat16)
             store = pltpu.make_async_copy(result.at[at, :], out_ref.at[at, :], out_sem.at[i])
             store.start()
             stores.append(store)
         for store in stores:
             store.wait()
 
-
-def chain(width, turn, deal, six, parts, before=()):
+    @pl.when(was_ahead)
+    def _():
+        form(1)
+
+    @pl.when(jnp.logical_not(was_ahead))
+    def _():
+        form(0)
+
+
+def chain(width, deal, six, parts, formed):
     cols = six.shape[0]
     shares = len(parts)
-    step = min(256, cols)
     any_space = pl.BlockSpec(memory_space=pl.ANY)
-    scratch = pltpu.VMEM((cols, cols), jnp.bfloat16)
-    return pl.pallas_call(
-        functools.partial(chain_kernel, width, turn, shares),
+    return pl.pallas_call(
+        functools.partial(chain_kernel, width, shares),
         out_shape=jax.ShapeDtypeStruct((cols, cols), jnp.bfloat16),
-        in_specs=[any_space] * (2 + shares + len(before)),
+        in_specs=[any_space] * (3 + shares),
         out_specs=any_space,
-        input_output_aliases={2 + shares: 0} if before else {},
         scratch_shapes=[
-            scratch,
-            scratch,
-            scratch,
+            pltpu.VMEM((cols, cols), jnp.bfloat16),
+            pltpu.VMEM((shares,) + parts[0].shape, jnp.bfloat16),
+            pltpu.VMEM((cols, cols), jnp.float32),
+            pltpu.VMEM((cols, cols), jnp.bfloat16),
             pltpu.SMEM((cols // width,), jnp.int32),
             pltpu.SemaphoreType.DMA,
             pltpu.SemaphoreType.DMA((cols // width,)),
             pltpu.SemaphoreType.DMA((shares,)),
-            pltpu.SemaphoreType.DMA((cols // step,)),
+            pltpu.SemaphoreType.DMA,
+            pltpu.SemaphoreType.DMA((cols // min(256, cols),)),
         ],
         cost_estimate=pl.CostEstimate(
             flops=6 * cols**3, bytes_accessed=6 * cols * cols, transcendentals=0
         ),
-    )(deal, six, *parts, *before)
+    )(deal, six, *parts, formed)
 
 
 def near_kernel(far_ref, near_ref, sem):
@@ -235,12 +321,12 @@
     width = cols // groups
     parts = panel_parts(interaction[0])
     outgoing = scatter(width, pandya_map, rows_live, amps[0])
-    both = chain(width, FIRST_TURN, deal, six_j[0], parts)
-    outgoing, both = lax.optimization_barrier((outgoing, both))
+    formed = ahead(width, len(parts), deal, six_j[0], parts[0])
+    outgoing, formed, *parts = lax.optimization_barrier((outgoing, formed, *parts))
     incoming = lax.all_to_all(
         outgoing.reshape(groups, width, rows), "chan", split_axis=0, concat_axis=0, tiled=True
     )
-    both = chain(width, 1 - FIRST_TURN, deal, six_j[0], parts, (both,))
+    both = chain(width, deal, six_j[0], parts, formed)
     both = near(both)
     sending = jnp.dot(
         both, incoming.reshape(cols, rows), preferred_element_type=jnp.float32

time: 65.6 us -> 65 us (level)
  Pallas kernels: 14.8 us -> 23.6 us
  waiting for transfers between devices: 13.8 us -> 5.31 us
  local copies, waits for them, and re-layouts: 2.56 us -> 1.6 us
    pallas_call x2, Pallas kernels: 10.4 us -> 19.3 us  [the longest x1 10.1 us: ahead(): pl.pallas_call(functools.partial(ahead_kernel, width, shares), out_shape=...]
    all_to_all x1, waiting for transfers between devices: 13.8 us -> 5.31 us  [per_device(): lax.all_to_all(outgoing.reshape(groups, width, rows), 'chan', split_axis=...]
    unnamed x8, local copies, waits for them, and re-layouts: 2.56 us -> 1.6 us
  transfers between devices with their start and end apart: 2 -> 2, of which waited for: 1 -> 1; matrix products, arithmetic and copies ran while one was open for 0% -> 0% of each run, Pallas kernels for 5% -> 34%
where the time goes in v5:
time: 65 us; the launch traced here: 64.7 us
  blocking collectives  24.3 us (37%)
  Pallas kernels  23.6 us (36%)
  starting transfers between devices  8.32 us (13%)
  waiting for transfers between devices  5.31 us (8%)
  local copies, waits for them, and re-layouts  1.6 us (2%)
  matrix products  1.24 us (2%)
    all_to_all x1, blocking collectives, per_device(): lax.all_to_all(sending.reshape(groups, width, rows), 'chan', split_axis=0...  24.3 us
    pallas_call x1, Pallas kernels, ahead(): pl.pallas_call(functools.partial(ahead_kernel, width, shares), out_shape=...  10.1 us
    pallas_call x1, Pallas kernels, chain(): pl.pallas_call(functools.partial(chain_kernel, width, shares), out_shape=...  9.18 us
    all_to_all x1, starting transfers between devices, per_device(): lax.all_to_all(outgoing.reshape(groups, width, rows), 'chan', split_axis=...  7.86 us
    all_to_all x1, waiting for transfers between devices, per_device(): lax.all_to_all(outgoing.reshape(groups, width, rows), 'chan', split_axis=...  5.31 us
    pallas_call x1, Pallas kernels, scatter(): pl.pallas_call(functools.partial(scatter_kernel, width), out_shape=jax.Sh...  2.5 us
    pallas_call x1, Pallas kernels, gather(): pl.pallas_call(functools.partial(gather_kernel, width), out_shape=jax.Sha...  1.67 us
    unnamed x8, local copies, waits for them, and re-layouts  1.6 us
  transfers between devices with their start and end apart: 2, of which 1 were waited for; matrix products, arithmetic and copies ran while one was open for 0% of the time, Pallas kernels for 34%

profile of v5, /device:TPU:0, one launch (start us, length us, event | category | flops | bytes accessed | tf_op | source)
XLA Modules:
  0.0 64.7 jit_solution(10642872963255865713)
XLA Ops:
  0.0 0.5 collective-permute-start
  0.5 2.5 %shard_map.64 = bf16[1024,512]{1,0:T(8,128)(2,1)} custom-call(s32[16]{0:T(128)} %map_ref.3, s32[16]{0:T(128)} %live_ref.3, bf16[512,1024]{1,0:T(8,128)(2,1)} %bitcast.13), custom_call_target="tpu_custom_call" | custom-call | bytes 2097152 | tf_op jit(solution)/shard_map/pallas_call | solution.py:81
  3.0 10.1 %shard_map.65.refs_4_ = f32[1024,1024]{1,0:T(8,128)} custom-call(s32[16]{0:T(128)} %refs_0_.1, bf16[1024,1024]{1,0:T(8,128)(2,1)} %bitcast.14, bf16[512,1024]{1,0:T(8,128)(2,1)} %bitcast.17), custom_call_target="tpu_custom_call" | custom-call | flops 2147483648 | bytes 8388608 | tf_op jit(solution)/shard_map/pallas_call | solution.py:193
  13.1 0.0 collective-permute-done.refs_3_
  13.1 0.0 copy-start.3
  13.1 7.9 %all-to-all-start = ((bf16[16,64,512]{2,1,0:T(8,128)(2,1)}), bf16[16,64,512]{2,1,0:T(8,128)(2,1)S(1)}, u32[]{:S(2)}, u32[]{:S(2)}) async-start(bf16[16,64,512]{2,1,0:T(8,128)(2,1)} %bitcast.3), calls=%async_computation | async-start | bytes 2097152 | tf_op jit(solution)/shard_map/all_to_all | solution.py:326
  21.0 0.0 copy-done.3
  21.0 9.2 %shard_map.66.far_ref = bf16[1024,1024]{1,0:T(8,128)(2,1)} custom-call(s32[16]{0:T(128)} %refs_0_.1, bf16[1024,1024]{1,0:T(8,128)(2,1)} %bitcast.15, bf16[512,1024]{1,0:T(8,128)(2,1)} %bitcast.18, bf16[512,1024]{1,0:T(8,128)(2,1)} %copy-done.3, f32[1024,1024]{1,0:T(8,128)} %shard_map.65.refs_4_), custom_call_target="tpu_custom_call" | custom-call | flops 6442450944 | bytes 6291456 | tf_op jit(solution)/shard_map/pallas_call | solution.py:266
  30.2 0.0 copy-start
  30.2 1.6 %copy-done = bf16[1024,1024]{1,0:T(8,128)(2,1)S(1)} copy-done((bf16[1024,1024]{1,0:T(8,128)(2,1)S(1)}, bf16[1024,1024]{1,0:T(8,128)(2,1)}, u32[]{:S(2)}) %copy-start) | copy-done | bytes 2097176
  31.8 0.1 shard_map.67
  31.9 5.3 %all-to-all-done = bf16[16,64,512]{2,1,0:T(8,128)(2,1)S(1)} async-done(((bf16[16,64,512]{2,1,0:T(8,128)(2,1)}), bf16[16,64,512]{2,1,0:T(8,128)(2,1)S(1)}, u32[]{:S(2)}, u32[]{:S(2)}) %all-to-all-start) | async-done | bytes 1048608 | tf_op jit(solution)/shard_map/all_to_all | solution.py:326
  37.2 1.2 %convolution_convert_fusion = bf16[1024,512]{1,0:T(8,128)(2,1)S(1)} fusion(bf16[1024,1024]{1,0:T(8,128)(2,1)S(1)} %shard_map.67, bf16[1024,512]{1,0:T(8,128)(2,1)S(1)} %bitcast.11), kind=kOutput, calls=%fused_computation | convolution fusion | flops 1074266112 | bytes 4194304 | tf_op jit(solution)/shard_map/dot_general | solution.py:331
  38.5 0.0 copy-start.1
  38.5 0.0 copy-start.2
  38.5 24.3 %all_to_all.10 = bf16[16,64,512]{2,1,0:T(8,128)(2,1)S(1)} all-to-all(bf16[16,64,512]{2,1,0:T(8,128)(2,1)S(1)} %bitcast.12), channel_id=1, replica_groups=mesh['chan'=16,'blk'=2] {'chan'}, dimensions={0} | all-to-all | bytes 2097152 | tf_op jit(solution)/shard_map/all_to_all | solution.py:334
  62.8 0.0 copy-done.1
  62.8 0.0 copy-done.2
  62.8 1.7 %shard_map.68 = bf16[512,1024]{1,0:T(8,128)(2,1)} custom-call(s32[16]{0:T(128)S(1)} %copy-done.1, s32[16]{0:T(128)S(1)} %copy-done.2, bf16[1024,512]{1,0:T(8,128)(2,1)S(1)} %bitcast.10), custom_call_target="tpu_custom_call" | custom-call | bytes 2097152 | tf_op jit(solution)/shard_map/pallas_call | solution.py:103
Async XLA Ops:
  0.0 13.1 %collective-permute-start = (bf16[512,1024]{1,0:T(8,128)(2,1)}, bf16[512,1024]{1,0:T(8,128)(2,1)S(1)}, u32[]{:S(2)}, u32[]{:S(2)}) collective-permute-start(bf16[512,1024]{1,0:T(8,128)(2,1)} %bitcast.16), channel_id=1, source_target_pairs={{0,1},{1,0},{2,3},{3,2},{4,5},{5,4},{6,7},{7,6},{8,9},{9,8},{10,11... | collective-permute-start | bytes 3145736 | tf_op jit(solution)/shard_map/ppermute | solution.py:313
  13.1 7.9 %copy-start.3 = (bf16[512,1024]{1,0:T(8,128)(2,1)}, bf16[512,1024]{1,0:T(8,128)(2,1)S(1)}, u32[]{:S(2)}) copy-start(bf16[512,1024]{1,0:T(8,128)(2,1)S(1)} %collective-permute-done.refs_3_) | copy-start | bytes 3145732
  13.1 24.1 %all-to-all-start = ((bf16[16,64,512]{2,1,0:T(8,128)(2,1)}), bf16[16,64,512]{2,1,0:T(8,128)(2,1)S(1)}, u32[]{:S(2)}, u32[]{:S(2)}) async-start(bf16[16,64,512]{2,1,0:T(8,128)(2,1)} %bitcast.3), calls=%async_computation | async-start | bytes 2097152 | tf_op jit(solution)/shard_map/all_to_all | solution.py:326
  30.2 1.6 %copy-start = (bf16[1024,1024]{1,0:T(8,128)(2,1)S(1)}, bf16[1024,1024]{1,0:T(8,128)(2,1)}, u32[]{:S(2)}) copy-start(bf16[1024,1024]{1,0:T(8,128)(2,1)} %shard_map.66.far_ref) | copy-start | bytes 6291460
  38.5 24.4 %copy-start.1 = (s32[16]{0:T(128)S(1)}, s32[16]{0:T(128)}, u32[]{:S(2)}) copy-start(s32[16]{0:T(128)} %map_ref.3) | copy-start | bytes 196
  38.5 24.4 %copy-start.2 = (s32[16]{0:T(128)S(1)}, s32[16]{0:T(128)}, u32[]{:S(2)}) copy-start(s32[16]{0:T(128)} %live_ref.3) | copy-start | bytes 196

commit v6 on v5

--- a/solution.py
+++ b/solution.py
@@ -9,7 +9,26 @@
 
 LANES = 128
 AHEAD = 0
+RANK_BITS = (3, 2, 0, 1)
 TERMS = 3
+
+
+def rank_bits(groups):
+    return RANK_BITS if groups == 1 << len(RANK_BITS) else range((groups - 1).bit_length())
+
+
+def ranks(groups):
+    if groups & (groups - 1):
+        return list(range(groups))
+    bits = rank_bits(groups)
+    return [sum(((r >> i) & 1) << bit for i, bit in enumerate(bits)) for r in range(groups)]
+
+
+def rank_of(place, groups):
+    if groups & (groups - 1):
+        return place
+    bits = rank_bits(groups)
+    return sum(((place >> bit) & 1) << i for i, bit in enumerate(bits))
 
 
 def live_lanes(first, rows, live):
@@ -41,7 +60,7 @@
         load.wait()
         turned[pl.ds(j * LANES, LANES), :] = jnp.where(keep, tile[j].T, 0)
         for k in range(j * per_tile, (j + 1) * per_tile):
-            at = pl.multiple_of(map_in[k] * width, width)
+            at = pl.multiple_of(rank_of(map_in[k], cols // width) * width, width)
             store = pltpu.make_async_copy(
                 turned.at[pl.ds(k * width, width), :],
                 out_ref.at[pl.ds(at, width), :],
@@ -63,7 +82,8 @@
     for j in range(cols // LANES):
         blocks = []
         for i in range(per_tile):
-            at = pl.multiple_of(map_ref[j * per_tile + i] * width, width)
+            rank = rank_of(map_ref[j * per_tile + i], cols // width)
+            at = pl.multiple_of(rank * width, width)
             blocks.append(back_ref[pl.ds(at, width), :])
         tile[j] = jnp.where(keep, jnp.concatenate(blocks, axis=0), 0).T
         store = pltpu.make_async_copy(
@@ -140,10 +160,10 @@
     blocks = [
         pltpu.make_async_copy(
             six_ref.at[pl.ds(pl.multiple_of(deal[s] * width, width), width), :],
-            six.at[pl.ds(s * width, width), :],
-            six_sem.at[s],
+            six.at[pl.ds(r * width, width), :],
+            six_sem.at[r],
         )
-        for s in range(six.shape[0] // width)
+        for r, s in enumerate(ranks(six.shape[0] // width))
     ]
     for copy in blocks:
         copy.start()
@@ -315,6 +335,14 @@
     return parts
 
 
+def exchange(block, groups):
+    parts = block.reshape(groups, block.shape[0] // groups, block.shape[1])
+    parts = lax.all_to_all(
+        parts, "chan", split_axis=0, concat_axis=0, tiled=True, axis_index_groups=[ranks(groups)]
+    )
+    return parts.reshape(block.shape)
+
+
 def per_device(amps, six_j, interaction, deal, pandya_map, rows_live):
     groups = lax.axis_size("chan")
     _, rows, cols = amps.shape
@@ -323,18 +351,12 @@
     outgoing = scatter(width, pandya_map, rows_live, amps[0])
     formed = ahead(width, len(parts), deal, six_j[0], parts[0])
     outgoing, formed, *parts = lax.optimization_barrier((outgoing, formed, *parts))
-    incoming = lax.all_to_all(
-        outgoing.reshape(groups, width, rows), "chan", split_axis=0, concat_axis=0, tiled=True
-    )
+    incoming = exchange(outgoing, groups)
     both = chain(width, deal, six_j[0], parts, formed)
     both = near(both)
-    sending = jnp.dot(
-        both, incoming.reshape(cols, rows), preferred_element_type=jnp.float32
-    ).astype(jnp.bfloat16)
-    arriving = lax.all_to_all(
-        sending.reshape(groups, width, rows), "chan", split_axis=0, concat_axis=0, tiled=True
-    )
-    result = gather(width, pandya_map, rows_live, arriving.reshape(cols, rows))
+    sending = jnp.dot(both, incoming, preferred_element_type=jnp.float32).astype(jnp.bfloat16)
+    arriving = exchange(sending, groups)
+    result = gather(width, pandya_map, rows_live, arriving)
     return result[None]
 
 

time: 65 us -> 62.3 us (0.958)
  blocking collectives: 24.3 us -> 21.3 us
    all_to_all x1, blocking collectives: 24.3 us -> 21.3 us  [exchange(): lax.all_to_all(parts, 'chan', split_axis=0, concat_axis=0, tiled=True, ax...]
  transfers between devices with their start and end apart: 2 -> 2, of which waited for: 1 -> 1; matrix products, arithmetic and copies ran while one was open for 0% -> 0% of each run, Pallas kernels for 34% -> 35%
where the time goes in v6:
time: 62.3 us; the launch traced here: 62 us
  Pallas kernels  23.6 us (38%)
  blocking collectives  21.3 us (34%)
  starting transfers between devices  8.33 us (13%)
  waiting for transfers between devices  5.61 us (9%)
  local copies, waits for them, and re-layouts  1.6 us (3%)
  matrix products  1.25 us (2%)
    all_to_all x1, blocking collectives, exchange(): lax.all_to_all(parts, 'chan', split_axis=0, concat_axis=0, tiled=True, ax...  21.3 us
    pallas_call x1, Pallas kernels, ahead(): pl.pallas_call(functools.partial(ahead_kernel, width, shares), out_shape=...  10.1 us
    pallas_call x1, Pallas kernels, chain(): pl.pallas_call(functools.partial(chain_kernel, width, shares), out_shape=...  9.18 us
    all_to_all x1, starting transfers between devices, exchange(): lax.all_to_all(parts, 'chan', split_axis=0, concat_axis=0, tiled=True, ax...  7.88 us
    all_to_all x1, waiting for transfers between devices, exchange(): lax.all_to_all(parts, 'chan', split_axis=0, concat_axis=0, tiled=True, ax...  5.61 us
    pallas_call x1, Pallas kernels, scatter(): pl.pallas_call(functools.partial(scatter_kernel, width), out_shape=jax.Sh...  2.52 us
    pallas_call x1, Pallas kernels, gather(): pl.pallas_call(functools.partial(gather_kernel, width), out_shape=jax.Sha...  1.67 us
    unnamed x8, local copies, waits for them, and re-layouts  1.6 us
  transfers between devices with their start and end apart: 2, of which 1 were waited for; matrix products, arithmetic and copies ran while one was open for 0% of the time, Pallas kernels for 35%

profile of v6, /device:TPU:0, one launch (start us, length us, event | category | flops | bytes accessed | tf_op | source)
XLA Modules:
  0.0 62.0 jit_solution(17261454740838517288)
XLA Ops:
  0.0 0.5 collective-permute-start
  0.5 2.5 %shard_map.64 = bf16[1024,512]{1,0:T(8,128)(2,1)} custom-call(s32[16]{0:T(128)} %map_ref.3, s32[16]{0:T(128)} %live_ref.3, bf16[512,1024]{1,0:T(8,128)(2,1)} %bitcast.13), custom_call_target="tpu_custom_call" | custom-call | bytes 2097152 | tf_op jit(solution)/shard_map/pallas_call | solution.py:101
  3.0 10.1 %shard_map.65.refs_4_ = f32[1024,1024]{1,0:T(8,128)} custom-call(s32[16]{0:T(128)} %refs_0_.1, bf16[1024,1024]{1,0:T(8,128)(2,1)} %bitcast.14, bf16[512,1024]{1,0:T(8,128)(2,1)} %bitcast.17), custom_call_target="tpu_custom_call" | custom-call | flops 2147483648 | bytes 8388608 | tf_op jit(solution)/shard_map/pallas_call | solution.py:213
  13.1 0.0 collective-permute-done.refs_3_
  13.1 0.0 copy-start.3
  13.1 7.9 %all-to-all-start = ((bf16[16,64,512]{2,1,0:T(8,128)(2,1)}), bf16[16,64,512]{2,1,0:T(8,128)(2,1)S(1)}, u32[]{:S(2)}, u32[]{:S(2)}) async-start(bf16[16,64,512]{2,1,0:T(8,128)(2,1)} %bitcast.3), calls=%async_computation | async-start | bytes 2097152 | tf_op jit(solution)/shard_map/all_to_all | solution.py:340
  21.0 0.0 copy-done.3
  21.0 9.2 %shard_map.66.far_ref = bf16[1024,1024]{1,0:T(8,128)(2,1)} custom-call(s32[16]{0:T(128)} %refs_0_.1, bf16[1024,1024]{1,0:T(8,128)(2,1)} %bitcast.15, bf16[512,1024]{1,0:T(8,128)(2,1)} %bitcast.18, bf16[512,1024]{1,0:T(8,128)(2,1)} %copy-done.3, f32[1024,1024]{1,0:T(8,128)} %shard_map.65.refs_4_), custom_call_target="tpu_custom_call" | custom-call | flops 6442450944 | bytes 6291456 | tf_op jit(solution)/shard_map/pallas_call | solution.py:286
  30.2 0.0 copy-start
  30.2 1.6 %copy-done = bf16[1024,1024]{1,0:T(8,128)(2,1)S(1)} copy-done((bf16[1024,1024]{1,0:T(8,128)(2,1)S(1)}, bf16[1024,1024]{1,0:T(8,128)(2,1)}, u32[]{:S(2)}) %copy-start) | copy-done | bytes 2097176
  31.8 0.1 shard_map.67
  31.9 5.6 %all-to-all-done = bf16[16,64,512]{2,1,0:T(8,128)(2,1)S(1)} async-done(((bf16[16,64,512]{2,1,0:T(8,128)(2,1)}), bf16[16,64,512]{2,1,0:T(8,128)(2,1)S(1)}, u32[]{:S(2)}, u32[]{:S(2)}) %all-to-all-start) | async-done | bytes 1048608 | tf_op jit(solution)/shard_map/all_to_all | solution.py:340
  37.6 1.3 %convolution_convert_fusion = bf16[1024,512]{1,0:T(8,128)(2,1)S(1)} fusion(bf16[1024,1024]{1,0:T(8,128)(2,1)S(1)} %shard_map.67, bf16[1024,512]{1,0:T(8,128)(2,1)S(1)} %bitcast.11), kind=kOutput, calls=%fused_computation | convolution fusion | flops 1074266112 | bytes 4194304 | tf_op jit(solution)/shard_map/dot_general | solution.py:357
  38.8 0.0 copy-start.1
  38.8 0.0 copy-start.2
  38.8 21.3 %all_to_all.10 = bf16[16,64,512]{2,1,0:T(8,128)(2,1)S(1)} all-to-all(bf16[16,64,512]{2,1,0:T(8,128)(2,1)S(1)} %bitcast.12), channel_id=1, replica_groups={{0,16,8,24,2,18,10,26,4,20,12,28,6,22,14,30},{1,17,9,25,3,19,11,27,5,21..., dimensions={0} | all-to-all | bytes 2097152 | tf_op jit(solution)/shard_map/all_to_all | solution.py:340
  60.1 0.0 copy-done.1
  60.1 0.0 copy-done.2
  60.1 1.7 %shard_map.68 = bf16[512,1024]{1,0:T(8,128)(2,1)} custom-call(s32[16]{0:T(128)S(1)} %copy-done.1, s32[16]{0:T(128)S(1)} %copy-done.2, bf16[1024,512]{1,0:T(8,128)(2,1)S(1)} %bitcast.10), custom_call_target="tpu_custom_call" | custom-call | bytes 2097152 | tf_op jit(solution)/shard_map/pallas_call | solution.py:123
Async XLA Ops:
  0.0 13.1 %collective-permute-start = (bf16[512,1024]{1,0:T(8,128)(2,1)}, bf16[512,1024]{1,0:T(8,128)(2,1)S(1)}, u32[]{:S(2)}, u32[]{:S(2)}) collective-permute-start(bf16[512,1024]{1,0:T(8,128)(2,1)} %bitcast.16), channel_id=1, source_target_pairs={{0,1},{1,0},{2,3},{3,2},{4,5},{5,4},{6,7},{7,6},{8,9},{9,8},{10,11... | collective-permute-start | bytes 3145736 | tf_op jit(solution)/shard_map/ppermute | solution.py:333
  13.1 7.9 %copy-start.3 = (bf16[512,1024]{1,0:T(8,128)(2,1)}, bf16[512,1024]{1,0:T(8,128)(2,1)S(1)}, u32[]{:S(2)}) copy-start(bf16[512,1024]{1,0:T(8,128)(2,1)S(1)} %collective-permute-done.refs_3_) | copy-start | bytes 3145732
  13.1 24.4 %all-to-all-start = ((bf16[16,64,512]{2,1,0:T(8,128)(2,1)}), bf16[16,64,512]{2,1,0:T(8,128)(2,1)S(1)}, u32[]{:S(2)}, u32[]{:S(2)}) async-start(bf16[16,64,512]{2,1,0:T(8,128)(2,1)} %bitcast.3), calls=%async_computation | async-start | bytes 2097152 | tf_op jit(solution)/shard_map/all_to_all | solution.py:340
  30.2 1.6 %copy-start = (bf16[1024,1024]{1,0:T(8,128)(2,1)S(1)}, bf16[1024,1024]{1,0:T(8,128)(2,1)}, u32[]{:S(2)}) copy-start(bf16[1024,1024]{1,0:T(8,128)(2,1)} %shard_map.66.far_ref) | copy-start | bytes 6291460
  38.8 21.3 %copy-start.1 = (s32[16]{0:T(128)S(1)}, s32[16]{0:T(128)}, u32[]{:S(2)}) copy-start(s32[16]{0:T(128)} %map_ref.3) | copy-start | bytes 196
  38.8 21.3 %copy-start.2 = (s32[16]{0:T(128)S(1)}, s32[16]{0:T(128)}, u32[]{:S(2)}) copy-start(s32[16]{0:T(128)} %live_ref.3) | copy-start | bytes 196

commit v7 on v6

--- a/solution.py
+++ b/solution.py
@@ -9,26 +9,23 @@
 
 LANES = 128
 AHEAD = 0
-RANK_BITS = (3, 2, 0, 1)
+RANKS = (9, 13, 8, 6, 10, 2, 14, 11, 12, 1, 0, 3, 15, 5, 4, 7)
 TERMS = 3
 
 
-def rank_bits(groups):
-    return RANK_BITS if groups == 1 << len(RANK_BITS) else range((groups - 1).bit_length())
-
-
 def ranks(groups):
-    if groups & (groups - 1):
-        return list(range(groups))
-    bits = rank_bits(groups)
-    return [sum(((r >> i) & 1) << bit for i, bit in enumerate(bits)) for r in range(groups)]
+    return list(RANKS) if groups == len(RANKS) else list(range(groups))
 
 
 def rank_of(place, groups):
-    if groups & (groups - 1):
+    if groups != len(RANKS):
         return place
-    bits = rank_bits(groups)
-    return sum(((place >> bit) & 1) << i for i, bit in enumerate(bits))
+    words = [0, 0]
+    for rank, at in enumerate(RANKS):
+        words[at // 8] |= rank << (at % 8 * 4)
+    low, high = (jnp.int32(word - (word >> 31 << 32)) for word in words)
+    word = jnp.where(place < 8, low, high)
+    return lax.shift_right_logical(word, (place & 7) * 4) & 15
 
 
 def live_lanes(first, rows, live):

time: 62.3 us -> 60.5 us (0.971)
  waiting for transfers between devices: 5.61 us -> 2.74 us
    all_to_all x1, waiting for transfers between devices: 5.61 us -> 2.74 us  [exchange(): lax.all_to_all(parts, 'chan', split_axis=0, concat_axis=0, tiled=True, ax...]
  transfers between devices with their start and end apart: 2 -> 2, of which waited for: 1 -> 1; matrix products, arithmetic and copies ran while one was open for 0% -> 0% of each run, Pallas kernels for 35% -> 36%
where the time goes in v7:
time: 60.5 us; the launch traced here: 60.2 us
  Pallas kernels  23.6 us (39%)
  blocking collectives  21.9 us (36%)
  starting transfers between devices  8.8 us (15%)
  waiting for transfers between devices  2.74 us (5%)
  local copies, waits for them, and re-layouts  1.6 us (3%)
  matrix products  1.24 us (2%)
    all_to_all x1, blocking collectives, exchange(): lax.all_to_all(parts, 'chan', split_axis=0, concat_axis=0, tiled=True, ax...  21.9 us
    pallas_call x1, Pallas kernels, ahead(): pl.pallas_call(functools.partial(ahead_kernel, width, shares), out_shape=...  10.1 us
    pallas_call x1, Pallas kernels, chain(): pl.pallas_call(functools.partial(chain_kernel, width, shares), out_shape=...  9.19 us
    all_to_all x1, starting transfers between devices, exchange(): lax.all_to_all(parts, 'chan', split_axis=0, concat_axis=0, tiled=True, ax...  8.35 us
    all_to_all x1, waiting for transfers between devices, exchange(): lax.all_to_all(parts, 'chan', split_axis=0, concat_axis=0, tiled=True, ax...  2.74 us
    pallas_call x1, Pallas kernels, scatter(): pl.pallas_call(functools.partial(scatter_kernel, width), out_shape=jax.Sh...  2.52 us
    pallas_call x1, Pallas kernels, gather(): pl.pallas_call(functools.partial(gather_kernel, width), out_shape=jax.Sha...  1.67 us
    unnamed x8, local copies, waits for them, and re-layouts  1.6 us
  transfers between devices with their start and end apart: 2, of which 1 were waited for; matrix products, arithmetic and copies ran while one was open for 0% of the time, Pallas kernels for 36%

profile of v7, /device:TPU:0, one launch (start us, length us, event | category | flops | bytes accessed | tf_op | source)
XLA Modules:
  0.0 60.2 jit_solution(11680668262768523076)
XLA Ops:
  0.0 0.5 collective-permute-start
  0.5 2.5 %shard_map.64 = bf16[1024,512]{1,0:T(8,128)(2,1)} custom-call(s32[16]{0:T(128)} %map_ref.3, s32[16]{0:T(128)} %live_ref.3, bf16[512,1024]{1,0:T(8,128)(2,1)} %bitcast.13), custom_call_target="tpu_custom_call" | custom-call | bytes 2097152 | tf_op jit(solution)/shard_map/pallas_call | solution.py:98
  3.0 10.1 %shard_map.65.refs_4_ = f32[1024,1024]{1,0:T(8,128)} custom-call(s32[16]{0:T(128)} %refs_0_.1, bf16[1024,1024]{1,0:T(8,128)(2,1)} %bitcast.14, bf16[512,1024]{1,0:T(8,128)(2,1)} %bitcast.17), custom_call_target="tpu_custom_call" | custom-call | flops 2147483648 | bytes 8388608 | tf_op jit(solution)/shard_map/pallas_call | solution.py:210
  13.1 0.0 collective-permute-done.refs_3_
  13.1 0.0 copy-start.3
  13.1 8.3 %all-to-all-start = ((bf16[16,64,512]{2,1,0:T(8,128)(2,1)}), bf16[16,64,512]{2,1,0:T(8,128)(2,1)S(1)}, u32[]{:S(2)}, u32[]{:S(2)}) async-start(bf16[16,64,512]{2,1,0:T(8,128)(2,1)} %bitcast.3), calls=%async_computation | async-start | bytes 2097152 | tf_op jit(solution)/shard_map/all_to_all | solution.py:337
  21.5 0.0 copy-done.3
  21.5 9.2 %shard_map.66.far_ref = bf16[1024,1024]{1,0:T(8,128)(2,1)} custom-call(s32[16]{0:T(128)} %refs_0_.1, bf16[1024,1024]{1,0:T(8,128)(2,1)} %bitcast.15, bf16[512,1024]{1,0:T(8,128)(2,1)} %bitcast.18, bf16[512,1024]{1,0:T(8,128)(2,1)} %copy-done.3, f32[1024,1024]{1,0:T(8,128)} %shard_map.65.refs_4_), custom_call_target="tpu_custom_call" | custom-call | flops 6442450944 | bytes 6291456 | tf_op jit(solution)/shard_map/pallas_call | solution.py:283
  30.7 0.0 copy-start
  30.7 1.6 %copy-done = bf16[1024,1024]{1,0:T(8,128)(2,1)S(1)} copy-done((bf16[1024,1024]{1,0:T(8,128)(2,1)S(1)}, bf16[1024,1024]{1,0:T(8,128)(2,1)}, u32[]{:S(2)}) %copy-start) | copy-done | bytes 2097176
  32.3 0.1 shard_map.67
  32.4 2.7 %all-to-all-done = bf16[16,64,512]{2,1,0:T(8,128)(2,1)S(1)} async-done(((bf16[16,64,512]{2,1,0:T(8,128)(2,1)}), bf16[16,64,512]{2,1,0:T(8,128)(2,1)S(1)}, u32[]{:S(2)}, u32[]{:S(2)}) %all-to-all-start) | async-done | bytes 1048608 | tf_op jit(solution)/shard_map/all_to_all | solution.py:337
  35.2 1.2 %convolution_convert_fusion = bf16[1024,512]{1,0:T(8,128)(2,1)S(1)} fusion(bf16[1024,1024]{1,0:T(8,128)(2,1)S(1)} %shard_map.67, bf16[1024,512]{1,0:T(8,128)(2,1)S(1)} %bitcast.11), kind=kOutput, calls=%fused_computation | convolution fusion | flops 1074266112 | bytes 4194304 | tf_op jit(solution)/shard_map/dot_general | solution.py:354
  36.4 0.0 copy-start.1
  36.4 0.0 copy-start.2
  36.4 21.9 %all_to_all.10 = bf16[16,64,512]{2,1,0:T(8,128)(2,1)S(1)} all-to-all(bf16[16,64,512]{2,1,0:T(8,128)(2,1)S(1)} %bitcast.12), channel_id=1, replica_groups={{18,26,16,12,20,4,28,22,24,2,0,6,30,10,8,14},{19,27,17,13,21,5,29,23,25..., dimensions={0} | all-to-all | bytes 2097152 | tf_op jit(solution)/shard_map/all_to_all | solution.py:337
  58.3 0.0 copy-done.1
  58.3 0.0 copy-done.2
  58.3 1.7 %shard_map.68 = bf16[512,1024]{1,0:T(8,128)(2,1)} custom-call(s32[16]{0:T(128)S(1)} %copy-done.1, s32[16]{0:T(128)S(1)} %copy-done.2, bf16[1024,512]{1,0:T(8,128)(2,1)S(1)} %bitcast.10), custom_call_target="tpu_custom_call" | custom-call | bytes 2097152 | tf_op jit(solution)/shard_map/pallas_call | solution.py:120
Async XLA Ops:
  0.0 13.1 %collective-permute-start = (bf16[512,1024]{1,0:T(8,128)(2,1)}, bf16[512,1024]{1,0:T(8,128)(2,1)S(1)}, u32[]{:S(2)}, u32[]{:S(2)}) collective-permute-start(bf16[512,1024]{1,0:T(8,128)(2,1)} %bitcast.16), channel_id=1, source_target_pairs={{0,1},{1,0},{2,3},{3,2},{4,5},{5,4},{6,7},{7,6},{8,9},{9,8},{10,11... | collective-permute-start | bytes 3145736 | tf_op jit(solution)/shard_map/ppermute | solution.py:330
  13.1 8.4 %copy-start.3 = (bf16[512,1024]{1,0:T(8,128)(2,1)}, bf16[512,1024]{1,0:T(8,128)(2,1)S(1)}, u32[]{:S(2)}) copy-start(bf16[512,1024]{1,0:T(8,128)(2,1)S(1)} %collective-permute-done.refs_3_) | copy-start | bytes 3145732
  13.1 22.0 %all-to-all-start = ((bf16[16,64,512]{2,1,0:T(8,128)(2,1)}), bf16[16,64,512]{2,1,0:T(8,128)(2,1)S(1)}, u32[]{:S(2)}, u32[]{:S(2)}) async-start(bf16[16,64,512]{2,1,0:T(8,128)(2,1)} %bitcast.3), calls=%async_computation | async-start | bytes 2097152 | tf_op jit(solution)/shard_map/all_to_all | solution.py:337
  30.7 1.6 %copy-start = (bf16[1024,1024]{1,0:T(8,128)(2,1)S(1)}, bf16[1024,1024]{1,0:T(8,128)(2,1)}, u32[]{:S(2)}) copy-start(bf16[1024,1024]{1,0:T(8,128)(2,1)} %shard_map.66.far_ref) | copy-start | bytes 6291460
  36.4 21.9 %copy-start.1 = (s32[16]{0:T(128)S(1)}, s32[16]{0:T(128)}, u32[]{:S(2)}) copy-start(s32[16]{0:T(128)} %map_ref.3) | copy-start | bytes 196
  36.4 21.9 %copy-start.2 = (s32[16]{0:T(128)S(1)}, s32[16]{0:T(128)}, u32[]{:S(2)}) copy-start(s32[16]{0:T(128)} %live_ref.3) | copy-start | bytes 196

commit v8 on v7

--- a/solution.py
+++ b/solution.py
@@ -9,7 +9,7 @@
 
 LANES = 128
 AHEAD = 0
-RANKS = (9, 13, 8, 6, 10, 2, 14, 11, 12, 1, 0, 3, 15, 5, 4, 7)
+RANKS = (8, 13, 4, 0, 12, 10, 14, 9, 2, 6, 5, 1, 3, 11, 7, 15)
 TERMS = 3
 
 

time: 60.5 us -> 59.7 us (0.987)
  waiting for transfers between devices: 2.74 us -> 1.77 us
    all_to_all x1, waiting for transfers between devices: 2.74 us -> 1.77 us  [exchange(): lax.all_to_all(parts, 'chan', split_axis=0, concat_axis=0, tiled=True, ax...]
  transfers between devices with their start and end apart: 2 -> 2, of which waited for: 1 -> 1; matrix products, arithmetic and copies ran while one was open for 0% -> 0% of each run, Pallas kernels for 36% -> 37%
where the time goes in v8:
time: 59.7 us; the launch traced here: 59 us
  Pallas kernels  23.6 us (40%)
  blocking collectives  21.8 us (37%)
  starting transfers between devices  8.8 us (15%)
  waiting for transfers between devices  1.77 us (3%)
  local copies, waits for them, and re-layouts  1.6 us (3%)
  matrix products  1.25 us (2%)
    all_to_all x1, blocking collectives, exchange(): lax.all_to_all(parts, 'chan', split_axis=0, concat_axis=0, tiled=True, ax...  21.8 us
    pallas_call x1, Pallas kernels, ahead(): pl.pallas_call(functools.partial(ahead_kernel, width, shares), out_shape=...  10.1 us
    pallas_call x1, Pallas kernels, chain(): pl.pallas_call(functools.partial(chain_kernel, width, shares), out_shape=...  9.18 us
    all_to_all x1, starting transfers between devices, exchange(): lax.all_to_all(parts, 'chan', split_axis=0, concat_axis=0, tiled=True, ax...  8.34 us
    pallas_call x1, Pallas kernels, scatter(): pl.pallas_call(functools.partial(scatter_kernel, width), out_shape=jax.Sh...  2.5 us
    all_to_all x1, waiting for transfers between devices, exchange(): lax.all_to_all(parts, 'chan', split_axis=0, concat_axis=0, tiled=True, ax...  1.77 us
    pallas_call x1, Pallas kernels, gather(): pl.pallas_call(functools.partial(gather_kernel, width), out_shape=jax.Sha...  1.67 us
    unnamed x8, local copies, waits for them, and re-layouts  1.6 us
  transfers between devices with their start and end apart: 2, of which 1 were waited for; matrix products, arithmetic and copies ran while one was open for 0% of the time, Pallas kernels for 37%

profile of v8, /device:TPU:0, one launch (start us, length us, event | category | flops | bytes accessed | tf_op | source)
XLA Modules:
  0.0 59.0 jit_solution(1316313415165936959)
XLA Ops:
  0.0 0.5 collective-permute-start
  0.5 2.5 %shard_map.64 = bf16[1024,512]{1,0:T(8,128)(2,1)} custom-call(s32[16]{0:T(128)} %map_ref.3, s32[16]{0:T(128)} %live_ref.3, bf16[512,1024]{1,0:T(8,128)(2,1)} %bitcast.13), custom_call_target="tpu_custom_call" | custom-call | bytes 2097152 | tf_op jit(solution)/shard_map/pallas_call | solution.py:98
  3.0 10.1 %shard_map.65.refs_4_ = f32[1024,1024]{1,0:T(8,128)} custom-call(s32[16]{0:T(128)} %refs_0_.1, bf16[1024,1024]{1,0:T(8,128)(2,1)} %bitcast.14, bf16[512,1024]{1,0:T(8,128)(2,1)} %bitcast.17), custom_call_target="tpu_custom_call" | custom-call | flops 2147483648 | bytes 8388608 | tf_op jit(solution)/shard_map/pallas_call | solution.py:210
  13.1 0.0 collective-permute-done.refs_3_
  13.1 0.0 copy-start.3
  13.1 8.3 %all-to-all-start = ((bf16[16,64,512]{2,1,0:T(8,128)(2,1)}), bf16[16,64,512]{2,1,0:T(8,128)(2,1)S(1)}, u32[]{:S(2)}, u32[]{:S(2)}) async-start(bf16[16,64,512]{2,1,0:T(8,128)(2,1)} %bitcast.3), calls=%async_computation | async-start | bytes 2097152 | tf_op jit(solution)/shard_map/all_to_all | solution.py:337
  21.4 0.0 copy-done.3
  21.4 9.2 %shard_map.66.far_ref = bf16[1024,1024]{1,0:T(8,128)(2,1)} custom-call(s32[16]{0:T(128)} %refs_0_.1, bf16[1024,1024]{1,0:T(8,128)(2,1)} %bitcast.15, bf16[512,1024]{1,0:T(8,128)(2,1)} %bitcast.18, bf16[512,1024]{1,0:T(8,128)(2,1)} %copy-done.3, f32[1024,1024]{1,0:T(8,128)} %shard_map.65.refs_4_), custom_call_target="tpu_custom_call" | custom-call | flops 6442450944 | bytes 6291456 | tf_op jit(solution)/shard_map/pallas_call | solution.py:283
  30.6 0.0 copy-start
  30.6 1.6 %copy-done = bf16[1024,1024]{1,0:T(8,128)(2,1)S(1)} copy-done((bf16[1024,1024]{1,0:T(8,128)(2,1)S(1)}, bf16[1024,1024]{1,0:T(8,128)(2,1)}, u32[]{:S(2)}) %copy-start) | copy-done | bytes 2097176
  32.2 0.1 shard_map.67
  32.4 1.8 %all-to-all-done = bf16[16,64,512]{2,1,0:T(8,128)(2,1)S(1)} async-done(((bf16[16,64,512]{2,1,0:T(8,128)(2,1)}), bf16[16,64,512]{2,1,0:T(8,128)(2,1)S(1)}, u32[]{:S(2)}, u32[]{:S(2)}) %all-to-all-start) | async-done | bytes 1048608 | tf_op jit(solution)/shard_map/all_to_all | solution.py:337
  34.2 1.2 %convolution_convert_fusion = bf16[1024,512]{1,0:T(8,128)(2,1)S(1)} fusion(bf16[1024,1024]{1,0:T(8,128)(2,1)S(1)} %shard_map.67, bf16[1024,512]{1,0:T(8,128)(2,1)S(1)} %bitcast.11), kind=kOutput, calls=%fused_computation | convolution fusion | flops 1074266112 | bytes 4194304 | tf_op jit(solution)/shard_map/dot_general | solution.py:354
  35.4 0.0 copy-start.1
  35.4 0.0 copy-start.2
  35.4 21.8 %all_to_all.10 = bf16[16,64,512]{2,1,0:T(8,128)(2,1)S(1)} all-to-all(bf16[16,64,512]{2,1,0:T(8,128)(2,1)S(1)} %bitcast.12), channel_id=1, replica_groups={{16,26,8,0,24,20,28,18,4,12,10,2,6,22,14,30},{17,27,9,1,25,21,29,19,5,1..., dimensions={0} | all-to-all | bytes 2097152 | tf_op jit(solution)/shard_map/all_to_all | solution.py:337
  57.2 0.0 copy-done.1
  57.2 0.0 copy-done.2
  57.2 1.7 %shard_map.68 = bf16[512,1024]{1,0:T(8,128)(2,1)} custom-call(s32[16]{0:T(128)S(1)} %copy-done.1, s32[16]{0:T(128)S(1)} %copy-done.2, bf16[1024,512]{1,0:T(8,128)(2,1)S(1)} %bitcast.10), custom_call_target="tpu_custom_call" | custom-call | bytes 2097152 | tf_op jit(solution)/shard_map/pallas_call | solution.py:120
Async XLA Ops:
  0.0 13.1 %collective-permute-start = (bf16[512,1024]{1,0:T(8,128)(2,1)}, bf16[512,1024]{1,0:T(8,128)(2,1)S(1)}, u32[]{:S(2)}, u32[]{:S(2)}) collective-permute-start(bf16[512,1024]{1,0:T(8,128)(2,1)} %bitcast.16), channel_id=1, source_target_pairs={{0,1},{1,0},{2,3},{3,2},{4,5},{5,4},{6,7},{7,6},{8,9},{9,8},{10,11... | collective-permute-start | bytes 3145736 | tf_op jit(solution)/shard_map/ppermute | solution.py:330
  13.1 8.4 %copy-start.3 = (bf16[512,1024]{1,0:T(8,128)(2,1)}, bf16[512,1024]{1,0:T(8,128)(2,1)S(1)}, u32[]{:S(2)}) copy-start(bf16[512,1024]{1,0:T(8,128)(2,1)S(1)} %collective-permute-done.refs_3_) | copy-start | bytes 3145732
  13.1 21.1 %all-to-all-start = ((bf16[16,64,512]{2,1,0:T(8,128)(2,1)}), bf16[16,64,512]{2,1,0:T(8,128)(2,1)S(1)}, u32[]{:S(2)}, u32[]{:S(2)}) async-start(bf16[16,64,512]{2,1,0:T(8,128)(2,1)} %bitcast.3), calls=%async_computation | async-start | bytes 2097152 | tf_op jit(solution)/shard_map/all_to_all | solution.py:337
  30.6 1.6 %copy-start = (bf16[1024,1024]{1,0:T(8,128)(2,1)S(1)}, bf16[1024,1024]{1,0:T(8,128)(2,1)}, u32[]{:S(2)}) copy-start(bf16[1024,1024]{1,0:T(8,128)(2,1)} %shard_map.66.far_ref) | copy-start | bytes 6291460
  35.4 21.8 %copy-start.1 = (s32[16]{0:T(128)S(1)}, s32[16]{0:T(128)}, u32[]{:S(2)}) copy-start(s32[16]{0:T(128)} %map_ref.3) | copy-start | bytes 196
  35.4 21.8 %copy-start.2 = (s32[16]{0:T(128)S(1)}, s32[16]{0:T(128)}, u32[]{:S(2)}) copy-start(s32[16]{0:T(128)} %live_ref.3) | copy-start | bytes 196

commit v9 on v8

--- a/solution.py
+++ b/solution.py
@@ -82,12 +82,12 @@
             rank = rank_of(map_ref[j * per_tile + i], cols // width)
             at = pl.multiple_of(rank * width, width)
             blocks.append(back_ref[pl.ds(at, width), :])
-        tile[j] = jnp.where(keep, jnp.concatenate(blocks, axis=0), 0).T
-        store = pltpu.make_async_copy(
-            tile.at[j], out_ref.at[:, pl.ds(j * LANES, LANES)], sem.at[j]
-        )
-        store.start()
-        stores.append(store)
+        tile[:, pl.ds(j * LANES, LANES)] = jnp.where(keep, jnp.concatenate(blocks, axis=0), 0).T
+        if j % 2:
+            at = pl.ds((j - 1) * LANES, 2 * LANES)
+            store = pltpu.make_async_copy(tile.at[:, at], out_ref.at[:, at], sem.at[j // 2])
+            store.start()
+            stores.append(store)
     for store in stores:
         store.wait()
 
@@ -127,7 +127,7 @@
         ],
         out_specs=pl.BlockSpec(memory_space=pl.ANY),
         scratch_shapes=[
-            pltpu.VMEM((cols // LANES, rows, LANES), jnp.bfloat16),
+            pltpu.VMEM((rows, cols), jnp.bfloat16),
             pltpu.SemaphoreType.DMA((cols // LANES,)),
         ],
         compiler_params=pltpu.CompilerParams(vmem_limit_bytes=8 * 1024 * 1024),

time: 59.7 us -> 59.7 us (level)
  no operation moved by 1% of the time
where the time goes in v9:
time: 59.7 us; the launch traced here: 59.1 us
  Pallas kernels  23.7 us (40%)
  blocking collectives  21.8 us (37%)
  starting transfers between devices  8.8 us (15%)
  waiting for transfers between devices  1.77 us (3%)
  local copies, waits for them, and re-layouts  1.6 us (3%)
  matrix products  1.25 us (2%)
    all_to_all x1, blocking collectives, exchange(): lax.all_to_all(parts, 'chan', split_axis=0, concat_axis=0, tiled=True, ax...  21.8 us
    pallas_call x1, Pallas kernels, ahead(): pl.pallas_call(functools.partial(ahead_kernel, width, shares), out_shape=...  10.1 us
    pallas_call x1, Pallas kernels, chain(): pl.pallas_call(functools.partial(chain_kernel, width, shares), out_shape=...  9.18 us
    all_to_all x1, starting transfers between devices, exchange(): lax.all_to_all(parts, 'chan', split_axis=0, concat_axis=0, tiled=True, ax...  8.34 us
    pallas_call x1, Pallas kernels, scatter(): pl.pallas_call(functools.partial(scatter_kernel, width), out_shape=jax.Sh...  2.51 us
    all_to_all x1, waiting for transfers between devices, exchange(): lax.all_to_all(parts, 'chan', split_axis=0, concat_axis=0, tiled=True, ax...  1.77 us
    pallas_call x1, Pallas kernels, gather(): pl.pallas_call(functools.partial(gather_kernel, width), out_shape=jax.Sha...  1.72 us
    unnamed x8, local copies, waits for them, and re-layouts  1.6 us
  transfers between devices with their start and end apart: 2, of which 1 were waited for; matrix products, arithmetic and copies ran while one was open for 0% of the time, Pallas kernels for 37%

profile of v9, /device:TPU:0, one launch (start us, length us, event | category | flops | bytes accessed | tf_op | source)
XLA Modules:
  0.0 59.1 jit_solution(14538308688055869792)
XLA Ops:
  0.0 0.5 collective-permute-start
  0.5 2.5 %shard_map.64 = bf16[1024,512]{1,0:T(8,128)(2,1)} custom-call(s32[16]{0:T(128)} %map_ref.3, s32[16]{0:T(128)} %live_ref.3, bf16[512,1024]{1,0:T(8,128)(2,1)} %bitcast.13), custom_call_target="tpu_custom_call" | custom-call | bytes 2097152 | tf_op jit(solution)/shard_map/pallas_call | solution.py:98
  3.0 10.1 %shard_map.65.refs_4_ = f32[1024,1024]{1,0:T(8,128)} custom-call(s32[16]{0:T(128)} %refs_0_.1, bf16[1024,1024]{1,0:T(8,128)(2,1)} %bitcast.14, bf16[512,1024]{1,0:T(8,128)(2,1)} %bitcast.17), custom_call_target="tpu_custom_call" | custom-call | flops 2147483648 | bytes 8388608 | tf_op jit(solution)/shard_map/pallas_call | solution.py:210
  13.1 0.0 collective-permute-done.refs_3_
  13.1 0.0 copy-start.3
  13.1 8.3 %all-to-all-start = ((bf16[16,64,512]{2,1,0:T(8,128)(2,1)}), bf16[16,64,512]{2,1,0:T(8,128)(2,1)S(1)}, u32[]{:S(2)}, u32[]{:S(2)}) async-start(bf16[16,64,512]{2,1,0:T(8,128)(2,1)} %bitcast.3), calls=%async_computation | async-start | bytes 2097152 | tf_op jit(solution)/shard_map/all_to_all | solution.py:337
  21.5 0.0 copy-done.3
  21.5 9.2 %shard_map.66.far_ref = bf16[1024,1024]{1,0:T(8,128)(2,1)} custom-call(s32[16]{0:T(128)} %refs_0_.1, bf16[1024,1024]{1,0:T(8,128)(2,1)} %bitcast.15, bf16[512,1024]{1,0:T(8,128)(2,1)} %bitcast.18, bf16[512,1024]{1,0:T(8,128)(2,1)} %copy-done.3, f32[1024,1024]{1,0:T(8,128)} %shard_map.65.refs_4_), custom_call_target="tpu_custom_call" | custom-call | flops 6442450944 | bytes 6291456 | tf_op jit(solution)/shard_map/pallas_call | solution.py:283
  30.6 0.0 copy-start
  30.7 1.6 %copy-done = bf16[1024,1024]{1,0:T(8,128)(2,1)S(1)} copy-done((bf16[1024,1024]{1,0:T(8,128)(2,1)S(1)}, bf16[1024,1024]{1,0:T(8,128)(2,1)}, u32[]{:S(2)}) %copy-start) | copy-done | bytes 2097176
  32.2 0.1 shard_map.67
  32.4 1.8 %all-to-all-done = bf16[16,64,512]{2,1,0:T(8,128)(2,1)S(1)} async-done(((bf16[16,64,512]{2,1,0:T(8,128)(2,1)}), bf16[16,64,512]{2,1,0:T(8,128)(2,1)S(1)}, u32[]{:S(2)}, u32[]{:S(2)}) %all-to-all-start) | async-done | bytes 1048608 | tf_op jit(solution)/shard_map/all_to_all | solution.py:337
  34.2 1.2 %convolution_convert_fusion = bf16[1024,512]{1,0:T(8,128)(2,1)S(1)} fusion(bf16[1024,1024]{1,0:T(8,128)(2,1)S(1)} %shard_map.67, bf16[1024,512]{1,0:T(8,128)(2,1)S(1)} %bitcast.11), kind=kOutput, calls=%fused_computation | convolution fusion | flops 1074266112 | bytes 4194304 | tf_op jit(solution)/shard_map/dot_general | solution.py:354
  35.4 0.0 copy-start.1
  35.4 0.0 copy-start.2
  35.4 21.8 %all_to_all.10 = bf16[16,64,512]{2,1,0:T(8,128)(2,1)S(1)} all-to-all(bf16[16,64,512]{2,1,0:T(8,128)(2,1)S(1)} %bitcast.12), channel_id=1, replica_groups={{16,26,8,0,24,20,28,18,4,12,10,2,6,22,14,30},{17,27,9,1,25,21,29,19,5,1..., dimensions={0} | all-to-all | bytes 2097152 | tf_op jit(solution)/shard_map/all_to_all | solution.py:337
  57.2 0.0 copy-done.1
  57.2 0.0 copy-done.2
  57.2 1.7 %shard_map.68 = bf16[512,1024]{1,0:T(8,128)(2,1)} custom-call(s32[16]{0:T(128)S(1)} %copy-done.1, s32[16]{0:T(128)S(1)} %copy-done.2, bf16[1024,512]{1,0:T(8,128)(2,1)S(1)} %bitcast.10), custom_call_target="tpu_custom_call" | custom-call | bytes 2097152 | tf_op jit(solution)/shard_map/pallas_call | solution.py:120
Async XLA Ops:
  0.0 13.1 %collective-permute-start = (bf16[512,1024]{1,0:T(8,128)(2,1)}, bf16[512,1024]{1,0:T(8,128)(2,1)S(1)}, u32[]{:S(2)}, u32[]{:S(2)}) collective-permute-start(bf16[512,1024]{1,0:T(8,128)(2,1)} %bitcast.16), channel_id=1, source_target_pairs={{0,1},{1,0},{2,3},{3,2},{4,5},{5,4},{6,7},{7,6},{8,9},{9,8},{10,11... | collective-permute-start | bytes 3145736 | tf_op jit(solution)/shard_map/ppermute | solution.py:330
  13.1 8.4 %copy-start.3 = (bf16[512,1024]{1,0:T(8,128)(2,1)}, bf16[512,1024]{1,0:T(8,128)(2,1)S(1)}, u32[]{:S(2)}) copy-start(bf16[512,1024]{1,0:T(8,128)(2,1)S(1)} %collective-permute-done.refs_3_) | copy-start | bytes 3145732
  13.1 21.1 %all-to-all-start = ((bf16[16,64,512]{2,1,0:T(8,128)(2,1)}), bf16[16,64,512]{2,1,0:T(8,128)(2,1)S(1)}, u32[]{:S(2)}, u32[]{:S(2)}) async-start(bf16[16,64,512]{2,1,0:T(8,128)(2,1)} %bitcast.3), calls=%async_computation | async-start | bytes 2097152 | tf_op jit(solution)/shard_map/all_to_all | solution.py:337
  30.6 1.6 %copy-start = (bf16[1024,1024]{1,0:T(8,128)(2,1)S(1)}, bf16[1024,1024]{1,0:T(8,128)(2,1)}, u32[]{:S(2)}) copy-start(bf16[1024,1024]{1,0:T(8,128)(2,1)} %shard_map.66.far_ref) | copy-start | bytes 6291460
  35.4 21.8 %copy-start.1 = (s32[16]{0:T(128)S(1)}, s32[16]{0:T(128)}, u32[]{:S(2)}) copy-start(s32[16]{0:T(128)} %map_ref.3) | copy-start | bytes 196
  35.4 21.8 %copy-start.2 = (s32[16]{0:T(128)S(1)}, s32[16]{0:T(128)}, u32[]{:S(2)}) copy-start(s32[16]{0:T(128)} %live_ref.3) | copy-start | bytes 196
